TPU v7x, 256 devices: a whole 4x4x8 slice. The times are simulated.
256 devices in a mesh: gx: 8 (over y, core), gz: 32 (over z, x).
Axes of the slice: x: 4, y: 4, z: 8, core: 2. Of those that a mesh axis runs over, the one named last changes fastest.
Arguments:
- velocity: float32 [4, 12288, 8192], P(None, 'gx', 'gz'), may hold values from -6 to 6
Outputs:
- derivative_sum: float32 [4, 12288, 8192], P(None, 'gx', 'gz')
All inputs are finite; a program needn't handle non-finite values.
Results may differ from a plain program's by a relative error of at most 0.000054.
Values sent between devices are 32-bit elements; how exact they have to be, the bound alone decides.
No kernel may reach another device: no remote copies, remote signals or barrier semaphores. Data moves between devices by JAX's collectives and lax.ppermute only.
A program may use at most 64 MiB of HBM per device.

v0:
```python
import math

import jax
import jax.numpy as jnp
from jax import lax
from jax.sharding import PartitionSpec as P

alpha_coef = 1.0 / 3.0


def with_halo(value, sides, width):
    for axis, dim in sides:
        size, length = (lax.axis_size(axis), value.shape[dim])
        up = [(i, (i + 1) % size) for i in range(size)]
        down = [(j, i) for i, j in up]
        last = lax.slice_in_dim(value, length - width, length, axis=dim)
        leading = lax.slice_in_dim(value, 0, width, axis=dim)
        before = lax.ppermute(last, axis, up)
        after = lax.ppermute(leading, axis, down)
        value = jnp.concatenate([before, value, after], axis=dim)
    return value


def green_entries(row_index, col_index, size):
    ratio = (math.sqrt(5.0) - 3.0) / 2.0
    log_mag = math.log(-ratio)
    scale = 1.0 / ((1.0 + 2.0 * alpha_coef * ratio) * (1.0 - math.exp((2 * size + 2) * log_mag)))
    distance = jnp.abs(row_index - col_index)
    lower = jnp.minimum(row_index, col_index)
    upper = jnp.maximum(row_index, col_index)
    parity = 1.0 - 2.0 * (distance % 2).astype(jnp.float32)
    decay = jnp.exp(distance.astype(jnp.float32) * log_mag)
    near_wall = 1.0 - jnp.exp((2 * lower + 2).astype(jnp.float32) * log_mag)
    far_wall = 1.0 - jnp.exp((2 * (size - upper)).astype(jnp.float32) * log_mag)
    valid = (col_index >= 0) & (col_index < size)
    return jnp.where(valid, scale * parity * decay * near_wall * far_wall, 0.0)


def explicit_rhs(extended):
    count = extended.shape[1]
    return 7.0 / 9.0 * (extended[:, 3 : count - 1] - extended[:, 1 : count - 3]) + 1.0 / 36.0 * (
        extended[:, 4:] - extended[:, : count - 4]
    )


def local_solve(right_side):
    field_count, row_count, lane_count = right_side.shape
    index_rows = jnp.arange(row_count, dtype=jnp.int32)
    green_full = green_entries(index_rows[:, None], index_rows[None, :], row_count)
    return jnp.einsum("ij,fjz->fiz", green_full, right_side, precision=lax.Precision.HIGHEST)


def edge_values(right_all, row_count, taps):
    offsets = jnp.arange(taps, dtype=jnp.int32)
    tail_weights = green_entries(row_count - 1 + 0 * offsets, row_count - taps + offsets, row_count)
    head_weights = green_entries(0 * offsets, offsets, row_count)
    prev_last = jnp.einsum(
        "j,fjz->fz", tail_weights, right_all[:, :taps], precision=lax.Precision.HIGHEST
    )
    next_first = jnp.einsum(
        "j,fjz->fz", head_weights, right_all[:, row_count + taps :], precision=lax.Precision.HIGHEST
    )
    return (prev_last, next_first)


def on_device(velocity):
    row_count = velocity.shape[1]
    lane_count = velocity.shape[2]
    spanwise = with_halo(velocity, (("gz", 2),), 3)
    extended = with_halo(velocity, (("gx", 1),), 130)
    right_all = explicit_rhs(extended)
    right_side = right_all[:, 128 : 128 + row_count]
    partial_value = local_solve(right_side)
    prev_last, next_first = edge_values(right_all, row_count, 128)
    index_rows = jnp.arange(row_count, dtype=jnp.int32)
    first_column = green_entries(index_rows, 0 * index_rows, row_count)
    last_column = green_entries(index_rows, row_count - 1 + 0 * index_rows, row_count)
    coupling = alpha_coef * first_column[0]
    divisor = 1.0 - coupling * coupling
    head_here = (partial_value[:, 0] - coupling * prev_last) / divisor
    tail_prev = prev_last - coupling * head_here
    head_next = (next_first - coupling * partial_value[:, -1]) / divisor
    x_derivative = (
        partial_value
        - alpha_coef * first_column[None, :, None] * tail_prev[:, None, :]
        - alpha_coef * last_column[None, :, None] * head_next[:, None, :]
    )
    first = spanwise[:, :, 4 : lane_count + 4] - spanwise[:, :, 2 : lane_count + 2]
    second = spanwise[:, :, 5 : lane_count + 5] - spanwise[:, :, 1 : lane_count + 1]
    third = spanwise[:, :, 6:] - spanwise[:, :, :lane_count]
    z_derivative = 0.75 * first - 0.15 * second + 1.0 / 60.0 * third
    return x_derivative + z_derivative


def solution(mesh):
    return jax.shard_map(
        on_device,
        mesh=mesh,
        in_specs=(P(None, "gx", "gz"),),
        out_specs=P(None, "gx", "gz"),
        check_vma=False,
    )
```

profile of v0, /device:TPU:1, one launch (start us, length us, event | category | flops | bytes accessed | tf_op | source)
XLA Modules:
  0.0 110.0 jit_solution(10090458548299807426)
XLA Ops:
  0.0 1.3 %fusion.233 = (f32[4,130,256]{2,1,0:T(8,128)S(1)}, f32[4,130,256]{2,1,0:T(8,128)S(1)}) fusion(f32[4,1536,256]{2,1,0:T(8,128)} %param.1), kind=kLoop, calls=%fused_computation.261 | loop fusion | bytes 2129920 | tf_op jit(solution)/shard_map/slice | solution.py:17
  1.3 0.2 copy.39
  1.5 2.7 %collective-permute-start = (f32[4,130,256]{2,0,1:T(4,128)S(1)}, f32[4,130,256]{2,0,1:T(4,128)S(1)}, u32[]{:S(2)}, u32[]{:S(2)}) collective-permute-start(f32[4,130,256]{2,0,1:T(4,128)S(1)} %copy.39), channel_id=1, source_target_pairs={{0,32},{32,64},{64,96},{96,128},{128,160},{160,192},{192,224},{224... | collective-permute-start | bytes 1597448 | tf_op jit(solution)/shard_map/ppermute | solution.py:18
  4.2 0.2 copy.40
  4.4 0.6 collective-permute-start.1
  5.0 6.6 %copy.30 = f32[4,1536,256]{1,2,0:T(8,128)} copy(f32[4,1536,256]{2,1,0:T(8,128)} %param.1) | data formatting | bytes 12582912 | tf_op args[0]
  11.6 1.1 fusion.234
  12.6 7.3 %collective-permute-start.2 = (f32[4,1536,3]{1,2,0:T(4,128)S(1)}, f32[4,1536,3]{1,2,0:T(4,128)S(1)}, u32[]{:S(2)}, u32[]{:S(2)}) collective-permute-start(f32[4,1536,3]{1,2,0:T(4,128)S(1)} %get-tuple-element.9), channel_id=1, source_target_pairs={{1,0},{2,1},{3,2},{4,3},{5,4},{6,5},{7,6},{8,7},{9,8},{10,9},{11,1... | collective-permute-start | bytes 221192 | tf_op jit(solution)/shard_map/ppermute | solution.py:19
  19.9 0.0 collective-permute-start.3
  20.0 0.6 slice.92
  22.7 0.0 collective-permute-done
  22.7 0.4 copy.29
  23.0 0.0 collective-permute-done.1
  23.0 0.4 copy.31
  23.4 9.0 %concatenate.14 = f32[4,1796,256]{1,2,0:T(8,128)} concatenate(f32[4,130,256]{1,2,0:T(8,128)S(1)} %copy.29, f32[4,1536,256]{1,2,0:T(8,128)} %copy.30, f32[4,130,256]{1,2,0:T(8,128)S(1)} %copy.31), dimensions={1} | concatenate | bytes 14712832 | tf_op jit(solution)/shard_map/concatenate | solution.py:20
  32.4 0.0 slice-start
  32.4 13.7 %fusion.37 = f32[4,1792,256]{1,2,0:T(8,128)S(1)} fusion(f32[4,1796,256]{1,2,0:T(8,128)} %concatenate.14), kind=kLoop, calls=%fused_computation.42 | loop fusion | flops 9175040 | bytes 36700160 | tf_op jit(solution)/shard_map/add | solution.py:41
  46.2 0.5 fusion.69
  46.7 0.5 fusion.71
  47.2 0.0 slice-start.1
  47.2 48.5 %fusion.63 = f32[4,1536,256]{1,2,0:T(8,128)S(1)} fusion(pred[1536]{0:T(1024)(128)(4,1)S(1)} %iota_compare_fusion, f32[4,1792,256]{1,2,0:T(8,128)S(1)} %fusion.37), kind=kOutput, calls=%fused_computation.71 | convolution fusion | flops 29073604608 | bytes 12584960 | tf_op jit(solution)/shard_map/ij,fjz->fiz/dot_general | solution.py:50
  95.7 0.5 slice_reduce_fusion
  96.2 0.0 collective-permute-done.2
  96.2 0.0 collective-permute-done.3
  96.3 0.0 slice-done
  96.3 0.0 slice-done.1
  96.3 7.1 %fusion.44 = f32[4,1536,256]{1,2,0:T(8,128)} fusion(f32[4,1536,3]{1,2,0:T(4,128)S(1)} %collective-permute-done.3, f32[4,1536,3]{1,2,0:T(4,128)S(1)} %collective-permute-done.2, f32[4,1536,256]{1,2,0:T(8,128)S(1)} %bitcast.29, f32[4,1536,256]{1,2,0:T(8,128)S(1)} %fusion.63, f32[4,256]{1,0:T(4,128)S(1)} %get-tuple-element.11, f32[1536]{0:T(1024)S(1)} %get-tuple-element.13, ...), kind=kLoop, calls=%fused_computation.50 | loop fusion | flops 29884416 | bytes 19042304 | tf_op jit(solution)/shard_map/add | solution.py:92
  103.4 6.6 %copy.36 = f32[4,1536,256]{2,1,0:T(8,128)} copy(f32[4,1536,256]{1,2,0:T(8,128)} %fusion.44) | data formatting | bytes 12582912 | tf_op jit(solution)/shard_map/add | solution.py:92
  (5 shorter events, 0.1 us)
Async XLA Ops:
  1.5 21.1 %collective-permute-start = (f32[4,130,256]{2,0,1:T(4,128)S(1)}, f32[4,130,256]{2,0,1:T(4,128)S(1)}, u32[]{:S(2)}, u32[]{:S(2)}) collective-permute-start(f32[4,130,256]{2,0,1:T(4,128)S(1)} %copy.39), channel_id=1, source_target_pairs={{0,32},{32,64},{64,96},{96,128},{128,160},{160,192},{192,224},{224... | collective-permute-start | bytes 1597448 | tf_op jit(solution)/shard_map/ppermute | solution.py:18
  4.4 18.6 %collective-permute-start.1 = (f32[4,130,256]{2,0,1:T(4,128)S(1)}, f32[4,130,256]{2,0,1:T(4,128)S(1)}, u32[]{:S(2)}, u32[]{:S(2)}) collective-permute-start(f32[4,130,256]{2,0,1:T(4,128)S(1)} %copy.40), channel_id=1, source_target_pairs={{32,0},{64,32},{96,64},{128,96},{160,128},{192,160},{224,192},{0,2... | collective-permute-start | bytes 1597448 | tf_op jit(solution)/shard_map/ppermute | solution.py:19
  12.6 83.6 %collective-permute-start.2 = (f32[4,1536,3]{1,2,0:T(4,128)S(1)}, f32[4,1536,3]{1,2,0:T(4,128)S(1)}, u32[]{:S(2)}, u32[]{:S(2)}) collective-permute-start(f32[4,1536,3]{1,2,0:T(4,128)S(1)} %get-tuple-element.9), channel_id=1, source_target_pairs={{1,0},{2,1},{3,2},{4,3},{5,4},{6,5},{7,6},{8,7},{9,8},{10,9},{11,1... | collective-permute-start | bytes 221192 | tf_op jit(solution)/shard_map/ppermute | solution.py:19
  19.9 76.3 %collective-permute-start.3 = (f32[4,1536,3]{1,2,0:T(4,128)S(1)}, f32[4,1536,3]{1,2,0:T(4,128)S(1)}, u32[]{:S(2)}, u32[]{:S(2)}) collective-permute-start(f32[4,1536,3]{1,2,0:T(4,128)S(1)} %get-tuple-element.10), channel_id=1, source_target_pairs={{0,1},{1,2},{2,3},{3,4},{4,5},{5,6},{6,7},{7,8},{8,9},{9,10},{10,1... | collective-permute-start | bytes 221192 | tf_op jit(solution)/shard_map/ppermute | solution.py:18
  32.4 63.8 %slice-start = ((s8[6291456]{0:T(1024)(128)(4,1)}), s8[2097152]{0:T(1024)(128)(4,1)S(1)}, s32[]{:S(2)}) async-start(s8[6291456]{0:T(1024)(128)(4,1)} %bitcast.28), calls=%async_computation | async-start | bytes 4194304
  47.2 49.0 %slice-start.1 = ((s8[6291456]{0:T(1024)(128)(4,1)}), s8[4194304]{0:T(1024)(128)(4,1)S(1)}, s32[]{:S(2)}) async-start(s8[6291456]{0:T(1024)(128)(4,1)} %bitcast.28), calls=%async_computation.1 | async-start | bytes 8388608
where the time goes:
time: 110 us
  matrix products  49.5 us (45%)
  local copies, waits for them, and re-layouts  26.2 us (24%)
  other arithmetic  21.5 us (20%)
  starting transfers between devices  10.6 us (10%)
  between operations  2.2 us (2%)
    dot_general x1, matrix products, local_solve(): jnp.einsum('ij,fjz->fiz', green_full, right_side, precision=lax.Precision...  48.5 us
    add x1, other arithmetic, explicit_rhs(): 7.0 / 9.0 * (extended[:, 3:count - 1] - extended[:, 1:count - 3])  13.7 us
    concatenate x1, local copies, waits for them, and re-layouts, with_halo(): value = jnp.concatenate([before, value, after], axis=dim)  9.01 us
    ppermute x2, starting transfers between devices, with_halo(): after = lax.ppermute(leading, axis, down)  7.88 us
    add x1, other arithmetic, on_device(): return x_derivative + z_derivative  7.15 us
    unnamed x7, local copies, waits for them, and re-layouts  6.98 us
    add x1, local copies, waits for them, and re-layouts, on_device(): return x_derivative + z_derivative  6.56 us
    ppermute x2, starting transfers between devices, with_halo(): before = lax.ppermute(last, axis, up)  2.7 us
  transfers between devices with their start and end apart: 4, of which 0 were waited for; matrix products, arithmetic and copies ran while one was open for 75% of the time, Pallas kernels for 0%

commit v1 on v0

v1 whole, which is shorter than its diff:
```python
import math

import jax
import jax.numpy as jnp
import numpy as np
from jax import lax
from jax.experimental import pallas as pl
from jax.experimental.pallas import tpu as pltpu
from jax.sharding import PartitionSpec as P

FIELDS, ROWS, LANES = 4, 1536, 256
HALO = 24
PAD = HALO + ROWS + HALO
SUB = 8
CHUNK = ROWS // SUB
WARM = HALO - 2
TILE = 128
BLOCKS = ROWS // TILE
RATIO = (math.sqrt(5.0) - 3.0) / 2.0
KAPPA = -1.0 / (3.0 * RATIO)
NEAR = 7.0 / 9.0 / KAPPA
FAR = 1.0 / 36.0 / KAPPA
MIB = 1 << 20


def edge_matrices():
    def green(m):
        return RATIO ** np.abs(m) / (KAPPA * (1.0 - RATIO * RATIO))

    def weight(m):
        return 7.0 / 9.0 * (green(m + 1) - green(m - 1)) + 1.0 / 36.0 * (green(m + 2) - green(m - 2))

    here = np.arange(HALO)[:, None]
    there = np.arange(HALO)[None, :]
    top = weight(here - (there - HALO))
    bottom = weight(here - (there + HALO))
    return top.astype(np.float32), bottom.astype(np.float32)


def pack_kernel(v_hbm, pad, head, tail, first, last, sems):
    copies = []
    for f in range(FIELDS):
        for c in range(2):
            lanes = pl.ds(c * TILE, TILE)
            copy = pltpu.make_async_copy(v_hbm.at[f, :, lanes], pad.at[f, c, pl.ds(HALO, ROWS)], sems.at[f, c])
            copy.start()
            copies.append(copy)
    zeros = jnp.zeros((HALO, TILE), jnp.float32)
    for f in range(FIELDS):
        for c in range(2):
            pad[f, c, pl.ds(0, HALO)] = zeros
            pad[f, c, pl.ds(HALO + ROWS, HALO)] = zeros
    lane = lax.broadcasted_iota(jnp.int32, (TILE, TILE), 1)
    for f in range(FIELDS):
        for c in range(2):
            copies[2 * f + c].wait()
            head[pl.ds(f * HALO, HALO), c * TILE : (c + 1) * TILE] = pad[f, c, pl.ds(HALO, HALO)]
            tail[pl.ds(f * HALO, HALO), c * TILE : (c + 1) * TILE] = pad[f, c, pl.ds(ROWS, HALO)]
        for b in range(BLOCKS):
            rows = pl.ds(HALO + b * TILE, TILE)
            both = jnp.where(lane < 64, pad[f, 0, rows], pad[f, 1, rows])
            turned = both.T
            at = pl.ds((f * BLOCKS + b) * 4, 4)
            first[at] = turned[0:4]
            last[at] = turned[TILE - 4 :]


def difference_matrix():
    gap = lax.broadcasted_iota(jnp.int32, (LANES, LANES), 0) - lax.broadcasted_iota(
        jnp.int32, (LANES, LANES), 1
    )
    size = jnp.abs(gap)
    weight = jnp.where(size == 1, 45.0, jnp.where(size == 2, -9.0, jnp.where(size == 3, 1.0, 0.0)))
    return jnp.where(gap < 0, -weight, weight).astype(jnp.bfloat16)


def inner_kernel(pad, out, swept):
    unroll = 4
    for f in range(0, FIELDS, 2):
        chains = [(g, c) for g in (f, f + 1) for c in (0, 1)]

        def row(chain, k):
            g, c = chain
            return pad[g, c, pl.ds(k, SUB, stride=CHUNK)]

        def forward(step, carry):
            carry = list(carry)
            for u in range(unroll):
                k = step * unroll + u
                for n, chain in enumerate(chains):
                    back2, back1, here, ahead1, y = carry[n]
                    ahead2 = row(chain, k + 4)
                    y = RATIO * y + (NEAR * (ahead1 - back1) + FAR * (ahead2 - back2))
                    swept[n, pl.ds(pl.multiple_of(k * SUB, SUB), SUB)] = y
                    carry[n] = (back1, here, ahead1, ahead2, y)
            return tuple(carry)

        start = tuple(
            tuple(row(chain, j) for j in range(4)) + (jnp.zeros((SUB, TILE), jnp.float32),)
            for chain in chains
        )
        steps = WARM + CHUNK + WARM
        lax.fori_loop(0, steps // unroll, forward, start)

        def value(n, k):
            return swept[n, pl.ds(pl.multiple_of(k * SUB, SUB), SUB)]

        def warm(step, carry):
            k = steps - 1 - step
            return tuple(RATIO * carry[n] + value(n, k) for n in range(4))

        def backward(step, carry):
            carry = list(carry)
            for u in range(unroll):
                k = CHUNK - 1 - (step * unroll + u)
                for n, (g, c) in enumerate(chains):
                    carry[n] = RATIO * carry[n] + value(n, k + WARM)
                    out[g, c, pl.ds(k, SUB, stride=CHUNK)] = carry[n]
            return tuple(carry)

        zero = tuple(jnp.zeros((SUB, TILE), jnp.float32) for _ in chains)
        carry = lax.fori_loop(0, WARM, warm, zero, unroll=True)
        lax.fori_loop(0, CHUNK // unroll, backward, carry)

    matrix = difference_matrix()
    for f in range(FIELDS):
        for b in range(0, ROWS, 256):
            rows = pl.ds(HALO + b, 256)
            here = jnp.concatenate([pad[f, 0, rows], pad[f, 1, rows]], axis=1)
            high = here.astype(jnp.bfloat16)
            rest = here - high.astype(jnp.float32)
            middle = rest.astype(jnp.bfloat16)
            low = (rest - middle.astype(jnp.float32)).astype(jnp.bfloat16)
            total = jnp.dot(high, matrix, preferred_element_type=jnp.float32)
            total += jnp.dot(middle, matrix, preferred_element_type=jnp.float32)
            total += jnp.dot(low, matrix, preferred_element_type=jnp.float32)
            total = total * (1.0 / 60.0)
            out[f, 0, pl.ds(b, 256)] += total[:, 0:TILE]
            out[f, 1, pl.ds(b, 256)] += total[:, TILE:]


def edge_kernel(inner, before, after, left, right, top, bottom, out_hbm, work, sems):
    copies = []
    zeros = jnp.zeros((TILE - 8, TILE), jnp.float32)
    none = jnp.zeros((1, TILE), jnp.float32)
    lane = lax.broadcasted_iota(jnp.int32, (TILE, TILE), 1)
    for f in range(FIELDS):
        for b in range(BLOCKS):
            at = (f * BLOCKS + b) * 4
            l3, l2, l1 = (left[pl.ds(at + n, 1)] for n in (1, 2, 3))
            r1, r2, r3 = (right[pl.ds(at + n, 1)] for n in (0, 1, 2))
            low = jnp.concatenate(
                [
                    -0.75 * l1 + 0.15 * l2 - l3 * (1.0 / 60.0),
                    0.15 * l1 - l2 * (1.0 / 60.0),
                    l1 * (-1.0 / 60.0),
                    none,
                ]
            )
            high = jnp.concatenate(
                [
                    none,
                    r1 * (1.0 / 60.0),
                    -0.15 * r1 + r2 * (1.0 / 60.0),
                    0.75 * r1 - 0.15 * r2 + r3 * (1.0 / 60.0),
                ]
            )
            turned = jnp.concatenate([low, zeros, high]).T
            rows = pl.ds(b * TILE, TILE)
            work[f, 0, rows] = inner[f, 0, rows] + jnp.where(lane < 64, turned, 0.0)
            work[f, 1, rows] = inner[f, 1, rows] + jnp.where(lane < 64, 0.0, turned)
        halo = pl.ds(f * HALO, HALO)
        low = jnp.dot(
            top[...], before[halo], precision=lax.Precision.HIGHEST, preferred_element_type=jnp.float32
        )
        high = jnp.dot(
            bottom[...], after[halo], precision=lax.Precision.HIGHEST, preferred_element_type=jnp.float32
        )
        for c in range(2):
            lanes = pl.ds(c * TILE, TILE)
            work[f, c, pl.ds(0, HALO)] += low[:, c * TILE : (c + 1) * TILE]
            work[f, c, pl.ds(ROWS - HALO, HALO)] += high[:, c * TILE : (c + 1) * TILE]
            copy = pltpu.make_async_copy(work.at[f, c], out_hbm.at[f, :, lanes], sems.at[f, c])
            copy.start()
            copies.append(copy)
    for copy in copies:
        copy.wait()


def vmem_spec():
    return pl.BlockSpec(memory_space=pltpu.VMEM)


def any_spec():
    return pl.BlockSpec(memory_space=pl.ANY)


def pack(velocity):
    f32 = jnp.float32
    return pl.pallas_call(
        pack_kernel,
        out_shape=(
            pltpu.VMEM((FIELDS, 2, PAD, TILE), f32),
            pltpu.VMEM((FIELDS * HALO, LANES), f32),
            pltpu.VMEM((FIELDS * HALO, LANES), f32),
            pltpu.VMEM((FIELDS * BLOCKS * 4, TILE), f32),
            pltpu.VMEM((FIELDS * BLOCKS * 4, TILE), f32),
        ),
        in_specs=[any_spec()],
        out_specs=(vmem_spec(),) * 5,
        scratch_shapes=[pltpu.SemaphoreType.DMA((FIELDS, 2))],
        compiler_params=pltpu.CompilerParams(vmem_limit_bytes=16 * MIB),
        name="pack",
    )(pltpu.with_memory_space_constraint(velocity, pltpu.HBM))


def inner(pad):
    return pl.pallas_call(
        inner_kernel,
        out_shape=pltpu.VMEM((FIELDS, 2, ROWS, TILE), jnp.float32),
        in_specs=[vmem_spec()],
        out_specs=vmem_spec(),
        scratch_shapes=[pltpu.VMEM((4, (WARM + CHUNK + WARM) * SUB, TILE), jnp.float32)],
        compiler_params=pltpu.CompilerParams(vmem_limit_bytes=16 * MIB),
        cost_estimate=pl.CostEstimate(flops=10**9, bytes_accessed=12 * MIB, transcendentals=0),
        name="inner",
    )(pad)


def edges(partial, before, after, left, right):
    top, bottom = edge_matrices()
    return pl.pallas_call(
        edge_kernel,
        out_shape=jax.ShapeDtypeStruct((FIELDS, ROWS, LANES), jnp.float32),
        in_specs=[vmem_spec()] * 7,
        out_specs=any_spec(),
        scratch_shapes=[
            pltpu.VMEM((FIELDS, 2, ROWS, TILE), jnp.float32),
            pltpu.SemaphoreType.DMA((FIELDS, 2)),
        ],
        compiler_params=pltpu.CompilerParams(vmem_limit_bytes=24 * MIB),
        name="edges",
    )(pltpu.with_memory_space_constraint(partial, pltpu.VMEM), before, after, left, right, jnp.asarray(top), jnp.asarray(bottom))


def on_device(velocity):
    pad, head, tail, first, last = pack(velocity)
    size_x, size_z = lax.axis_size("gx"), lax.axis_size("gz")

    def shift(value, axis, size, by):
        return lax.ppermute(value, axis, [(i, (i + by) % size) for i in range(size)])

    left = shift(last, "gz", size_z, 1)
    right = shift(first, "gz", size_z, -1)
    before = shift(tail, "gx", size_x, 1)
    after = shift(head, "gx", size_x, -1)
    partial = inner(pltpu.with_memory_space_constraint(pad, pltpu.VMEM))
    return edges(partial, before, after, left, right)


def solution(mesh):
    return jax.shard_map(
        on_device,
        mesh=mesh,
        in_specs=(P(None, "gx", "gz"),),
        out_specs=P(None, "gx", "gz"),
        check_vma=False,
    )
```

time: 110 us -> 32.5 us (0.30)
  matrix products: 49.5 us -> 0 us
  local copies, waits for them, and re-layouts: 26.2 us -> 0.01 us
  Pallas kernels: 0 us -> 21.8 us
  other arithmetic: 21.5 us -> 0 us
  between operations: 2.2 us -> 0.07 us
    dot_general x3 -> x0, matrix products: 49.5 us -> none  [the longest x1 48.5 us: local_solve(): jnp.einsum('ij,fjz->fiz', green_full, right_side, precision=lax.Precision...]
    pallas_call x0 -> x3, Pallas kernels: none -> 21.8 us  [the longest x1 15.6 us: inner(): pl.pallas_call(inner_kernel, out_shape=pltpu.VMEM((FIELDS, 2, ROWS, TILE)...]
    add x2 -> x0, other arithmetic: 20.9 us -> none  [the longest x1 13.7 us: explicit_rhs(): 7.0 / 9.0 * (extended[:, 3:count - 1] - extended[:, 1:count - 3])]
    concatenate x1 -> x0, local copies, waits for them, and re-layouts: 9.01 us -> none  [with_halo(): value = jnp.concatenate([before, value, after], axis=dim)]
    unnamed x7 -> x4, local copies, waits for them, and re-layouts: 6.98 us -> 0.01 us
    add x1 -> x0, local copies, waits for them, and re-layouts: 6.56 us -> none  [on_device(): return x_derivative + z_derivative]
    slice x3 -> x0, local copies, waits for them, and re-layouts: 2.95 us -> none  [the longest x2 2.36 us: with_halo(): leading = lax.slice_in_dim(value, 0, width, axis=dim)]
  transfers between devices with their start and end apart: 4 -> 4, of which waited for: 0 -> 0; matrix products, arithmetic and copies ran while one was open for 75% -> 0% of each run, Pallas kernels for 0% -> 48%
where the time goes in v1:
time: 32.5 us; the launch traced here: 32.4 us
  Pallas kernels  21.8 us (67%)
  starting transfers between devices  10.5 us (32%)
    pallas_call x1, Pallas kernels, inner(): pl.pallas_call(inner_kernel, out_shape=pltpu.VMEM((FIELDS, 2, ROWS, TILE)...  15.6 us
    ppermute x4, starting transfers between devices, shift(): lax.ppermute(value, axis, [(i, (i + by) % size) for i in range(size)])  10.5 us
    pallas_call x1, Pallas kernels, pack(): pl.pallas_call(pack_kernel, out_shape=(pltpu.VMEM((FIELDS, 2, PAD, TILE),...  3.13 us
    pallas_call x1, Pallas kernels, edges(): pl.pallas_call(edge_kernel, out_shape=jax.ShapeDtypeStruct((FIELDS, ROWS,...  3.05 us
  transfers between devices with their start and end apart: 4, of which 0 were waited for; matrix products, arithmetic and copies ran while one was open for 0% of the time, Pallas kernels for 48%

profile of v1, /device:TPU:1, one launch (start us, length us, event | category | flops | bytes accessed | tf_op | source)
XLA Modules:
  0.0 32.4 jit_solution(15231596874797230079)
XLA Ops:
  0.0 3.1 %pack.1 = (f32[4,2,1584,128]{3,2,1,0:T(8,128)S(1)}, f32[96,256]{1,0:T(8,128)S(1)}, f32[96,256]{1,0:T(8,128)S(1)}, f32[192,128]{1,0:T(8,128)S(1)}, f32[192,128]{1,0:T(8,128)S(1)}) custom-call(f32[4,1536,256]{2,1,0:T(8,128)} %v_hbm.1), custom_call_target="tpu_custom_call" | custom-call | tf_op jit(solution)/shard_map/pack/pallas_call | solution.py:200
  3.1 2.7 %collective-permute-start = (f32[96,256]{1,0:T(8,128)S(1)}, f32[96,256]{1,0:T(8,128)S(1)}, u32[]{:S(2)}, u32[]{:S(2)}) collective-permute-start(f32[96,256]{1,0:T(8,128)S(1)} %get-tuple-element.11), channel_id=1, source_target_pairs={{0,32},{32,64},{64,96},{96,128},{128,160},{160,192},{192,224},{224... | collective-permute-start | bytes 294920 | tf_op jit(solution)/shard_map/ppermute | solution.py:251
  5.8 0.6 %collective-permute-start.1 = (f32[96,256]{1,0:T(8,128)S(1)}, f32[96,256]{1,0:T(8,128)S(1)}, u32[]{:S(2)}, u32[]{:S(2)}) collective-permute-start(f32[96,256]{1,0:T(8,128)S(1)} %get-tuple-element.12), channel_id=1, source_target_pairs={{0,224},{32,0},{64,32},{96,64},{128,96},{160,128},{192,160},{224,1... | collective-permute-start | bytes 294920 | tf_op jit(solution)/shard_map/ppermute | solution.py:251
  6.4 0.6 %collective-permute-start.2 = (f32[192,128]{1,0:T(8,128)S(1)}, f32[192,128]{1,0:T(8,128)S(1)}, u32[]{:S(2)}, u32[]{:S(2)}) collective-permute-start(f32[192,128]{1,0:T(8,128)S(1)} %get-tuple-element.13), channel_id=1, source_target_pairs={{0,1},{1,2},{2,3},{3,4},{4,5},{5,6},{6,7},{7,8},{8,9},{9,10},{10,1... | collective-permute-start | bytes 294920 | tf_op jit(solution)/shard_map/ppermute | solution.py:251
  7.1 6.6 %collective-permute-start.3 = (f32[192,128]{1,0:T(8,128)S(1)}, f32[192,128]{1,0:T(8,128)S(1)}, u32[]{:S(2)}, u32[]{:S(2)}) collective-permute-start(f32[192,128]{1,0:T(8,128)S(1)} %get-tuple-element.14), channel_id=1, source_target_pairs={{0,31},{1,0},{2,1},{3,2},{4,3},{5,4},{6,5},{7,6},{8,7},{9,8},{10,9... | collective-permute-start | bytes 294920 | tf_op jit(solution)/shard_map/ppermute | solution.py:251
  13.6 0.0 copy-start
  13.6 0.0 copy-start.1
  13.6 15.6 %inner.1 = f32[4,2,1536,128]{3,2,1,0:T(8,128)S(1)} custom-call(f32[4,2,1584,128]{3,2,1,0:T(8,128)S(1)} %get-tuple-element.10.pad), custom_call_target="tpu_custom_call" | custom-call | flops 1000000000 | bytes 12582912 | tf_op jit(solution)/shard_map/inner/pallas_call | solution.py:218
  29.3 0.0 collective-permute-done.before
  29.3 0.0 collective-permute-done.1.after
  29.3 0.0 collective-permute-done.2.left
  29.3 0.0 collective-permute-done.3.right
  29.3 0.0 copy-done
  29.3 0.0 copy-done.1
  29.3 3.0 %edges.1 = f32[4,1536,256]{2,1,0:T(8,128)} custom-call(f32[4,2,1536,128]{3,2,1,0:T(8,128)S(1)} %inner.1, f32[96,256]{1,0:T(8,128)S(1)} %collective-permute-done.before, f32[96,256]{1,0:T(8,128)S(1)} %collective-permute-done.1.after, f32[192,128]{1,0:T(8,128)S(1)} %collective-permute-done.2.left, f32[192,128]{1,0:T(8,128)S(1)} %collective-permute-done.3.right, ...), custom_call_target="tpu_custom_call" | custom-call | tf_op jit(solution)/shard_map/edges/pallas_call | solution.py:232
Async XLA Ops:
  3.1 26.1 %collective-permute-start = (f32[96,256]{1,0:T(8,128)S(1)}, f32[96,256]{1,0:T(8,128)S(1)}, u32[]{:S(2)}, u32[]{:S(2)}) collective-permute-start(f32[96,256]{1,0:T(8,128)S(1)} %get-tuple-element.11), channel_id=1, source_target_pairs={{0,32},{32,64},{64,96},{96,128},{128,160},{160,192},{192,224},{224... | collective-permute-start | bytes 294920 | tf_op jit(solution)/shard_map/ppermute | solution.py:251
  5.8 23.5 %collective-permute-start.1 = (f32[96,256]{1,0:T(8,128)S(1)}, f32[96,256]{1,0:T(8,128)S(1)}, u32[]{:S(2)}, u32[]{:S(2)}) collective-permute-start(f32[96,256]{1,0:T(8,128)S(1)} %get-tuple-element.12), channel_id=1, source_target_pairs={{0,224},{32,0},{64,32},{96,64},{128,96},{160,128},{192,160},{224,1... | collective-permute-start | bytes 294920 | tf_op jit(solution)/shard_map/ppermute | solution.py:251
  6.4 22.9 %collective-permute-start.2 = (f32[192,128]{1,0:T(8,128)S(1)}, f32[192,128]{1,0:T(8,128)S(1)}, u32[]{:S(2)}, u32[]{:S(2)}) collective-permute-start(f32[192,128]{1,0:T(8,128)S(1)} %get-tuple-element.13), channel_id=1, source_target_pairs={{0,1},{1,2},{2,3},{3,4},{4,5},{5,6},{6,7},{7,8},{8,9},{9,10},{10,1... | collective-permute-start | bytes 294920 | tf_op jit(solution)/shard_map/ppermute | solution.py:251
  7.1 22.3 %collective-permute-start.3 = (f32[192,128]{1,0:T(8,128)S(1)}, f32[192,128]{1,0:T(8,128)S(1)}, u32[]{:S(2)}, u32[]{:S(2)}) collective-permute-start(f32[192,128]{1,0:T(8,128)S(1)} %get-tuple-element.14), channel_id=1, source_target_pairs={{0,31},{1,0},{2,1},{3,2},{4,3},{5,4},{6,5},{7,6},{8,7},{9,8},{10,9... | collective-permute-start | bytes 294920 | tf_op jit(solution)/shard_map/ppermute | solution.py:251
  13.6 15.7 %copy-start = (f32[24,24]{1,0:T(8,128)S(1)}, f32[24,24]{1,0:T(8,128)}, u32[]{:S(2)}) copy-start(f32[24,24]{1,0:T(8,128)} %constant.5.clone.bottom) | copy-start | bytes 6916
  13.6 15.7 %copy-start.1 = (f32[24,24]{1,0:T(8,128)S(1)}, f32[24,24]{1,0:T(8,128)}, u32[]{:S(2)}) copy-start(f32[24,24]{1,0:T(8,128)} %constant.4.clone.top) | copy-start | bytes 6916

commit v2 on v1

v2 whole, which is shorter than its diff:
```python
import math

import jax
import jax.numpy as jnp
import numpy as np
from jax import lax
from jax.experimental import pallas as pl
from jax.experimental.pallas import tpu as pltpu
from jax.sharding import PartitionSpec as P

FIELDS, ROWS, LANES = 4, 1536, 256
HALO = 24
PAD = 1576
SUB = 8
CHUNK = ROWS // SUB + 1
WARM = HALO - 2
STEPS = 216
UNROLL = 8
EARLY = 2
LONG = SUB * CHUNK
TILE = 128
BLOCKS = ROWS // TILE
RATIO = (math.sqrt(5.0) - 3.0) / 2.0
KAPPA = -1.0 / (3.0 * RATIO)
NEAR = 7.0 / 9.0 / KAPPA
FAR = 1.0 / 36.0 / KAPPA
MIB = 1 << 20


def edge_matrices():
    def green(m):
        return RATIO ** np.abs(m) / (KAPPA * (1.0 - RATIO * RATIO))

    def weight(m):
        return 7.0 / 9.0 * (green(m + 1) - green(m - 1)) + 1.0 / 36.0 * (green(m + 2) - green(m - 2))

    here = np.arange(HALO)[:, None]
    there = np.arange(HALO)[None, :]
    top = weight(here - (there - HALO))
    bottom = weight(here - (there + HALO))
    return top.astype(np.float32), bottom.astype(np.float32)


def difference_matrix():
    gap = lax.broadcasted_iota(jnp.int32, (LANES, LANES), 0) - lax.broadcasted_iota(
        jnp.int32, (LANES, LANES), 1
    )
    size = jnp.abs(gap)
    weight = jnp.where(size == 1, 45.0, jnp.where(size == 2, -9.0, jnp.where(size == 3, 1.0, 0.0)))
    return jnp.where(gap < 0, -weight, weight).astype(jnp.bfloat16)


def spanwise(here, matrix):
    high = here.astype(jnp.bfloat16)
    rest = here - high.astype(jnp.float32)
    middle = rest.astype(jnp.bfloat16)
    low = (rest - middle.astype(jnp.float32)).astype(jnp.bfloat16)
    total = jnp.dot(high, matrix, preferred_element_type=jnp.float32)
    total += jnp.dot(middle, matrix, preferred_element_type=jnp.float32)
    total += jnp.dot(low, matrix, preferred_element_type=jnp.float32)
    return total * (1.0 / 60.0)


def field_rows(pad, f, row, count):
    rows = pl.ds(HALO + row, count)
    return jnp.concatenate([pad[f, 0, rows], pad[f, 1, rows]], axis=1)


def is_even(axis):
    return lax.rem(lax.axis_index(axis), 2) == 0


def pack_kernel(v_hbm, pad, z_part, near_x, far_x, near_z, far_z, sems):
    copies = []
    for f in range(FIELDS):
        for c in range(2):
            lanes = pl.ds(c * TILE, TILE)
            copy = pltpu.make_async_copy(v_hbm.at[f, :, lanes], pad.at[f, c, pl.ds(HALO, ROWS)], sems.at[f, c])
            copy.start()
            copies.append(copy)
    even_x, even_z = is_even("gx"), is_even("gz")
    matrix = difference_matrix()
    zeros = jnp.zeros((HALO, TILE), jnp.float32)
    for f in range(FIELDS):
        for c in range(2):
            pad[f, c, pl.ds(0, HALO)] = zeros
            pad[f, c, pl.ds(HALO + ROWS, PAD - HALO - ROWS)] = jnp.zeros((PAD - HALO - ROWS, TILE), jnp.float32)
    lane = lax.broadcasted_iota(jnp.int32, (TILE, TILE), 1)
    for f in range(FIELDS):
        for c in range(2):
            copies[2 * f + c].wait()
        for c in range(2):
            at, lanes = pl.ds(f * HALO, HALO), pl.ds(c * TILE, TILE)
            head, tail = pad[f, c, pl.ds(HALO, HALO)], pad[f, c, pl.ds(ROWS, HALO)]
            near_x[at, lanes] = jnp.where(even_x, tail, head)
            far_x[at, lanes] = jnp.where(even_x, head, tail)
        for b in range(BLOCKS):
            rows = pl.ds(HALO + b * TILE, TILE)
            turned = jnp.where(lane < 64, pad[f, 0, rows], pad[f, 1, rows]).T
            at = pl.ds((f * BLOCKS + b) * 4, 4)
            first, last = turned[0:4], turned[TILE - 4 :]
            near_z[at] = jnp.where(even_z, last, first)
            far_z[at] = jnp.where(even_z, first, last)
        if f < EARLY:
            for b in range(0, ROWS, 256):
                total = spanwise(field_rows(pad, f, b, 256), matrix)
                z_part[f, 0, pl.ds(b, 256)] = total[:, :TILE]
                z_part[f, 1, pl.ds(b, 256)] = total[:, TILE:]


def inner_kernel(pad, z_part, out, swept):
    chains = [(f, c) for f in range(FIELDS) for c in (0, 1)]
    count = len(chains)

    def row(chain, k):
        f, c = chain
        return pad[f, c, pl.ds(k, SUB, stride=CHUNK)]

    def forward(step, carry):
        carry = list(carry)
        for u in range(UNROLL):
            k = step * UNROLL + u
            for n, chain in enumerate(chains):
                back2, back1, here, ahead1, y = carry[n]
                ahead2 = row(chain, k + 4)
                y = RATIO * y + (NEAR * (ahead1 - back1) + FAR * (ahead2 - back2))
                swept[n, pl.ds(pl.multiple_of(k * SUB, SUB), SUB)] = y
                carry[n] = (back1, here, ahead1, ahead2, y)
        return tuple(carry)

    zero = jnp.zeros((SUB, TILE), jnp.float32)
    start = tuple(tuple(row(chain, j) for j in range(4)) + (zero,) for chain in chains)
    lax.fori_loop(0, STEPS // UNROLL, forward, start)

    def value(n, k):
        return swept[n, pl.ds(pl.multiple_of(k * SUB, SUB), SUB)]

    carry = [zero] * count
    for k in range(WARM - 1, -1, -1):
        carry = [RATIO * carry[n] + value(n, k + WARM) for n in range(count)]
    sub = lax.broadcasted_iota(jnp.int32, (SUB, TILE), 0)
    beyond = RATIO / (1.0 - RATIO * RATIO)
    carry = [
        jnp.where(sub == SUB - 1, beyond * value(n, WARM + CHUNK - 1), pltpu.roll(carry[n], SUB - 1, 0))
        for n in range(count)
    ]

    def back(carry, k):
        carry = [RATIO * carry[n] + value(n, k + WARM) for n in range(count)]
        for n, (f, c) in enumerate(chains):
            at = pl.ds(k, SUB, stride=CHUNK)
            out[f, c, at] = carry[n] + z_part[f, c, at] if f < EARLY else carry[n]
        return carry

    def backward(step, carry):
        for u in range(UNROLL):
            carry = back(carry, CHUNK - 2 - (step * UNROLL + u))
        return tuple(carry)

    lax.fori_loop(0, CHUNK // UNROLL, backward, tuple(back(carry, CHUNK - 1)))


def edge_kernel(pad, inner, near_x, far_x, near_z, far_z, top, bottom, out_hbm, work, sems):
    copies = []
    even_x, even_z = is_even("gx"), is_even("gz")
    matrix = difference_matrix()
    zeros = jnp.zeros((TILE - 8, TILE), jnp.float32)
    none = jnp.zeros((1, TILE), jnp.float32)
    lane = lax.broadcasted_iota(jnp.int32, (TILE, TILE), 1)
    for f in range(FIELDS):
        for b in range(BLOCKS):
            rows = pl.ds(b * TILE, TILE)
            at = pl.ds((f * BLOCKS + b) * 4, 4)
            near, far = near_z[at], far_z[at]
            left, right = jnp.where(even_z, far, near), jnp.where(even_z, near, far)
            l3, l2, l1 = (left[n : n + 1] for n in (1, 2, 3))
            r1, r2, r3 = (right[n : n + 1] for n in (0, 1, 2))
            low = jnp.concatenate(
                [
                    -0.75 * l1 + 0.15 * l2 - l3 * (1.0 / 60.0),
                    0.15 * l1 - l2 * (1.0 / 60.0),
                    l1 * (-1.0 / 60.0),
                    none,
                ]
            )
            high = jnp.concatenate(
                [
                    none,
                    r1 * (1.0 / 60.0),
                    -0.15 * r1 + r2 * (1.0 / 60.0),
                    0.75 * r1 - 0.15 * r2 + r3 * (1.0 / 60.0),
                ]
            )
            turned = jnp.concatenate([low, zeros, high]).T
            parts = [inner[f, c, rows] for c in range(2)]
            if f >= EARLY:
                total = spanwise(field_rows(pad, f, b * TILE, TILE), matrix)
                parts = [parts[c] + total[:, c * TILE : (c + 1) * TILE] for c in range(2)]
            work[f, 0, rows] = parts[0] + jnp.where(lane < 64, turned, 0.0)
            work[f, 1, rows] = parts[1] + jnp.where(lane < 64, 0.0, turned)
        halo = pl.ds(f * HALO, HALO)
        near, far = near_x[halo], far_x[halo]
        before, after = jnp.where(even_x, far, near), jnp.where(even_x, near, far)
        low = jnp.dot(top[...], before, precision=lax.Precision.HIGHEST, preferred_element_type=jnp.float32)
        high = jnp.dot(bottom[...], after, precision=lax.Precision.HIGHEST, preferred_element_type=jnp.float32)
        for c in range(2):
            lanes = pl.ds(c * TILE, TILE)
            work[f, c, pl.ds(0, HALO)] += low[:, c * TILE : (c + 1) * TILE]
            work[f, c, pl.ds(ROWS - HALO, HALO)] += high[:, c * TILE : (c + 1) * TILE]
            copy = pltpu.make_async_copy(work.at[f, c], out_hbm.at[f, :, lanes], sems.at[f, c])
            copy.start()
            copies.append(copy)
    for copy in copies:
        copy.wait()


def vmem_spec():
    return pl.BlockSpec(memory_space=pltpu.VMEM)


def any_spec():
    return pl.BlockSpec(memory_space=pl.ANY)


def in_vmem(value):
    return pltpu.with_memory_space_constraint(value, pltpu.VMEM)


def pack(velocity):
    f32 = jnp.float32
    return pl.pallas_call(
        pack_kernel,
        out_shape=(
            pltpu.VMEM((FIELDS, 2, PAD, TILE), f32),
            pltpu.VMEM((EARLY, 2, LONG, TILE), f32),
            pltpu.VMEM((FIELDS * HALO, LANES), f32),
            pltpu.VMEM((FIELDS * HALO, LANES), f32),
            pltpu.VMEM((FIELDS * BLOCKS * 4, TILE), f32),
            pltpu.VMEM((FIELDS * BLOCKS * 4, TILE), f32),
        ),
        in_specs=[any_spec()],
        out_specs=(vmem_spec(),) * 6,
        scratch_shapes=[pltpu.SemaphoreType.DMA((FIELDS, 2))],
        compiler_params=pltpu.CompilerParams(vmem_limit_bytes=16 * MIB),
        name="pack",
    )(pltpu.with_memory_space_constraint(velocity, pltpu.HBM))


def inner(pad, z_part):
    return pl.pallas_call(
        inner_kernel,
        out_shape=pltpu.VMEM((FIELDS, 2, LONG, TILE), jnp.float32),
        in_specs=[vmem_spec()] * 2,
        out_specs=vmem_spec(),
        scratch_shapes=[pltpu.VMEM((2 * FIELDS, STEPS * SUB, TILE), jnp.float32)],
        compiler_params=pltpu.CompilerParams(vmem_limit_bytes=16 * MIB),
        cost_estimate=pl.CostEstimate(flops=10**9, bytes_accessed=12 * MIB, transcendentals=0),
        name="inner",
    )(in_vmem(pad), in_vmem(z_part))


def edges(pad, partial, near_x, far_x, near_z, far_z):
    top, bottom = edge_matrices()
    return pl.pallas_call(
        edge_kernel,
        out_shape=jax.ShapeDtypeStruct((FIELDS, ROWS, LANES), jnp.float32),
        in_specs=[vmem_spec()] * 8,
        out_specs=any_spec(),
        scratch_shapes=[
            pltpu.VMEM((FIELDS, 2, ROWS, TILE), jnp.float32),
            pltpu.SemaphoreType.DMA((FIELDS, 2)),
        ],
        compiler_params=pltpu.CompilerParams(vmem_limit_bytes=16 * MIB),
        name="edges",
    )(in_vmem(pad), in_vmem(partial), near_x, far_x, near_z, far_z, jnp.asarray(top), jnp.asarray(bottom))


def on_device(velocity):
    pad, z_part, near_x, far_x, near_z, far_z = pack(velocity)

    def swap(value, axis, first):
        size = lax.axis_size(axis)
        pairs = [(i % size, (i + 1) % size) for i in range(first, size, 2)]
        return lax.ppermute(value, axis, pairs + [(j, i) for i, j in pairs])

    near_z, far_z = swap(near_z, "gz", 0), swap(far_z, "gz", 1)
    near_x, far_x = swap(near_x, "gx", 0), swap(far_x, "gx", 1)
    partial = inner(pad, z_part)
    return edges(pad, partial, near_x, far_x, near_z, far_z)


def solution(mesh):
    return jax.shard_map(
        on_device,
        mesh=mesh,
        in_specs=(P(None, "gx", "gz"),),
        out_specs=P(None, "gx", "gz"),
        check_vma=False,
    )
```

time: 32.5 us -> 21.2 us (0.65)
  Pallas kernels: 21.8 us -> 9.86 us
  starting transfers between devices: 10.5 us -> 11.2 us
    pallas_call x1, Pallas kernels: 15.6 us -> 3 us  [inner(): pl.pallas_call(inner_kernel, out_shape=pltpu.VMEM((FIELDS, 2, LONG, TILE)...]
    ppermute x4, starting transfers between devices: 10.5 us -> 11.2 us  [swap(): return lax.ppermute(value, axis, pairs + [(j, i) for i, j in pairs])]
    pallas_call x1, Pallas kernels: 3.13 us -> 3.58 us  [pack(): pl.pallas_call(pack_kernel, out_shape=(pltpu.VMEM((FIELDS, 2, PAD, TILE),...]
  transfers between devices with their start and end apart: 4 -> 4, of which waited for: 0 -> 0; matrix products, arithmetic and copies ran while one was open for 0% -> 0% of each run, Pallas kernels for 48% -> 14%
where the time goes in v2:
time: 21.2 us; the launch traced here: 21.1 us
  starting transfers between devices  11.2 us (53%)
  Pallas kernels  9.86 us (47%)
    ppermute x4, starting transfers between devices, swap(): return lax.ppermute(value, axis, pairs + [(j, i) for i, j in pairs])  11.2 us
    pallas_call x1, Pallas kernels, pack(): pl.pallas_call(pack_kernel, out_shape=(pltpu.VMEM((FIELDS, 2, PAD, TILE),...  3.58 us
    pallas_call x1, Pallas kernels, edges(): pl.pallas_call(edge_kernel, out_shape=jax.ShapeDtypeStruct((FIELDS, ROWS,...  3.29 us
    pallas_call x1, Pallas kernels, inner(): pl.pallas_call(inner_kernel, out_shape=pltpu.VMEM((FIELDS, 2, LONG, TILE)...  3 us
  transfers between devices with their start and end apart: 4, of which 0 were waited for; matrix products, arithmetic and copies ran while one was open for 0% of the time, Pallas kernels for 14%

profile of v2, /device:TPU:1, one launch (start us, length us, event | category | flops | bytes accessed | tf_op | source)
XLA Modules:
  0.0 21.1 jit_solution(3991029698748886135)
XLA Ops:
  0.0 3.6 %pack.1 = (f32[4,2,1576,128]{3,2,1,0:T(8,128)S(1)}, f32[2,2,1544,128]{3,2,1,0:T(8,128)S(1)}, f32[96,256]{1,0:T(8,128)S(1)}, f32[96,256]{1,0:T(8,128)S(1)}, f32[1...) custom-call(f32[4,1536,256]{2,1,0:T(8,128)} %v_hbm.1), custom_call_target="tpu_custom_call" | custom-call | tf_op jit(solution)/shard_map/pack/pallas_call | solution.py:231
  3.6 3.3 %collective-permute-start = (f32[96,256]{1,0:T(8,128)S(1)}, f32[96,256]{1,0:T(8,128)S(1)}, u32[]{:S(2)}, u32[]{:S(2)}) collective-permute-start(f32[96,256]{1,0:T(8,128)S(1)} %get-tuple-element.13), channel_id=1, source_target_pairs={{0,32},{64,96},{128,160},{192,224},{32,0},{96,64},{160,128},{224,1... | collective-permute-start | bytes 294920 | tf_op jit(solution)/shard_map/ppermute | solution.py:284
  6.9 0.0 collective-permute-start.1
  6.9 0.8 %collective-permute-start.2 = (f32[192,128]{1,0:T(8,128)S(1)}, f32[192,128]{1,0:T(8,128)S(1)}, u32[]{:S(2)}, u32[]{:S(2)}) collective-permute-start(f32[192,128]{1,0:T(8,128)S(1)} %get-tuple-element.15), channel_id=1, source_target_pairs={{0,1},{2,3},{4,5},{6,7},{8,9},{10,11},{12,13},{14,15},{16,17},{18,... | collective-permute-start | bytes 294920 | tf_op jit(solution)/shard_map/ppermute | solution.py:284
  7.7 7.1 %collective-permute-start.3 = (f32[192,128]{1,0:T(8,128)S(1)}, f32[192,128]{1,0:T(8,128)S(1)}, u32[]{:S(2)}, u32[]{:S(2)}) collective-permute-start(f32[192,128]{1,0:T(8,128)S(1)} %get-tuple-element.16), channel_id=1, source_target_pairs={{1,2},{3,4},{5,6},{7,8},{9,10},{11,12},{13,14},{15,16},{17,18},{19... | collective-permute-start | bytes 294920 | tf_op jit(solution)/shard_map/ppermute | solution.py:284
  14.8 0.0 copy-start
  14.8 0.0 copy-start.1
  14.8 3.0 %inner.1 = f32[4,2,1544,128]{3,2,1,0:T(8,128)S(1)} custom-call(f32[4,2,1576,128]{3,2,1,0:T(8,128)S(1)} %get-tuple-element.11.pad, f32[2,2,1544,128]{3,2,1,0:T(8,128)S(1)} %get-tuple-element.12.z_part), custom_call_target="tpu_custom_call" | custom-call | flops 1000000000 | bytes 12582912 | tf_op jit(solution)/shard_map/inner/pallas_call | solution.py:250
  17.8 0.0 collective-permute-done.near_x
  17.8 0.0 collective-permute-done.1.far_x
  17.8 0.0 collective-permute-done.2.near_z
  17.8 0.0 collective-permute-done.3.far_z
  17.8 0.0 copy-done
  17.8 0.0 copy-done.1
  17.8 3.3 %edges.1 = f32[4,1536,256]{2,1,0:T(8,128)} custom-call(f32[4,2,1576,128]{3,2,1,0:T(8,128)S(1)} %get-tuple-element.11.pad, f32[4,2,1544,128]{3,2,1,0:T(8,128)S(1)} %inner.1, f32[96,256]{1,0:T(8,128)S(1)} %collective-permute-done.near_x, f32[96,256]{1,0:T(8,128)S(1)} %collective-permute-done.1.far_x, f32[192,128]{1,0:T(8,128)S(1)} %collective-permute-done.2.near_z, ...), custom_call_target="tpu_custom_call" | custom-call | tf_op jit(solution)/shard_map/edges/pallas_call | solution.py:264
Async XLA Ops:
  3.6 14.2 %collective-permute-start = (f32[96,256]{1,0:T(8,128)S(1)}, f32[96,256]{1,0:T(8,128)S(1)}, u32[]{:S(2)}, u32[]{:S(2)}) collective-permute-start(f32[96,256]{1,0:T(8,128)S(1)} %get-tuple-element.13), channel_id=1, source_target_pairs={{0,32},{64,96},{128,160},{192,224},{32,0},{96,64},{160,128},{224,1... | collective-permute-start | bytes 294920 | tf_op jit(solution)/shard_map/ppermute | solution.py:284
  6.9 10.9 %collective-permute-start.1 = (f32[96,256]{1,0:T(8,128)S(1)}, f32[96,256]{1,0:T(8,128)S(1)}, u32[]{:S(2)}, u32[]{:S(2)}) collective-permute-start(f32[96,256]{1,0:T(8,128)S(1)} %get-tuple-element.14), channel_id=1, source_target_pairs={{32,64},{96,128},{160,192},{224,0},{64,32},{128,96},{192,160},{0,2... | collective-permute-start | bytes 294920 | tf_op jit(solution)/shard_map/ppermute | solution.py:284
  6.9 10.9 %collective-permute-start.2 = (f32[192,128]{1,0:T(8,128)S(1)}, f32[192,128]{1,0:T(8,128)S(1)}, u32[]{:S(2)}, u32[]{:S(2)}) collective-permute-start(f32[192,128]{1,0:T(8,128)S(1)} %get-tuple-element.15), channel_id=1, source_target_pairs={{0,1},{2,3},{4,5},{6,7},{8,9},{10,11},{12,13},{14,15},{16,17},{18,... | collective-permute-start | bytes 294920 | tf_op jit(solution)/shard_map/ppermute | solution.py:284
  7.7 10.1 %collective-permute-start.3 = (f32[192,128]{1,0:T(8,128)S(1)}, f32[192,128]{1,0:T(8,128)S(1)}, u32[]{:S(2)}, u32[]{:S(2)}) collective-permute-start(f32[192,128]{1,0:T(8,128)S(1)} %get-tuple-element.16), channel_id=1, source_target_pairs={{1,2},{3,4},{5,6},{7,8},{9,10},{11,12},{13,14},{15,16},{17,18},{19... | collective-permute-start | bytes 294920 | tf_op jit(solution)/shard_map/ppermute | solution.py:284
  14.8 3.0 %copy-start = (f32[24,24]{1,0:T(8,128)S(1)}, f32[24,24]{1,0:T(8,128)}, u32[]{:S(2)}) copy-start(f32[24,24]{1,0:T(8,128)} %constant.5.clone.bottom) | copy-start | bytes 6916
  14.8 3.1 %copy-start.1 = (f32[24,24]{1,0:T(8,128)S(1)}, f32[24,24]{1,0:T(8,128)}, u32[]{:S(2)}) copy-start(f32[24,24]{1,0:T(8,128)} %constant.4.clone.top) | copy-start | bytes 6916

commit v3 on v2

v3 whole, which is shorter than its diff:
```python
import math

import jax
import jax.numpy as jnp
import numpy as np
from jax import lax
from jax.experimental import pallas as pl
from jax.experimental.pallas import tpu as pltpu
from jax.sharding import PartitionSpec as P

FIELDS, ROWS, LANES = 4, 1536, 256
HALO = 24
PAD = 1576
SUB = 8
CHUNK = ROWS // SUB + 1
WARM = HALO - 2
STEPS = 216
UNROLL = 8
EARLY = 1
MIDDLE = 2
LONG = SUB * CHUNK
TILE = 128
BLOCKS = ROWS // TILE
TILE_ROWS = FIELDS * BLOCKS
RATIO = (math.sqrt(5.0) - 3.0) / 2.0
KAPPA = -1.0 / (3.0 * RATIO)
NEAR = 7.0 / 9.0 / KAPPA
FAR = 1.0 / 36.0 / KAPPA
MIB = 1 << 20


GAP = TILE_ROWS + 1
EDGE = 152
SCALE = 1.0 / (KAPPA * (1.0 - RATIO * RATIO))
TAIL = SCALE * (7.0 / 9.0 * (RATIO - 1.0 / RATIO) + 1.0 / 36.0 * (RATIO**2 - RATIO**-2))
NEXT = -1.0 / 12.0


def powers(exponent):
    value = jnp.where(exponent % 2 == 1, RATIO, 1.0)
    for bit in (2, 4, 8, 16):
        value = value * jnp.where((exponent // bit) % 2 == 1, RATIO**bit, 1.0)
    return value


def difference_matrix():
    gap = lax.broadcasted_iota(jnp.int32, (LANES, LANES), 0) - lax.broadcasted_iota(
        jnp.int32, (LANES, LANES), 1
    )
    size = jnp.abs(gap)
    weight = jnp.where(size == 1, 45.0, jnp.where(size == 2, -9.0, jnp.where(size == 3, 1.0, 0.0)))
    return jnp.where(gap < 0, -weight, weight).astype(jnp.bfloat16)


def spanwise(here, matrix):
    high = here.astype(jnp.bfloat16)
    rest = here - high.astype(jnp.float32)
    middle = rest.astype(jnp.bfloat16)
    low = (rest - middle.astype(jnp.float32)).astype(jnp.bfloat16)
    total = jnp.dot(high, matrix, preferred_element_type=jnp.float32)
    total += jnp.dot(middle, matrix, preferred_element_type=jnp.float32)
    total += jnp.dot(low, matrix, preferred_element_type=jnp.float32)
    return total * (1.0 / 60.0)


def field_rows(pad, f, row, count):
    rows = pl.ds(HALO + row, count)
    return jnp.concatenate([pad[f, 0, rows], pad[f, 1, rows]], axis=1)


def is_even(axis):
    return lax.rem(lax.axis_index(axis), 2) == 0


def pack_kernel(v_hbm, pad, z_part, near_x, far_x, near_z, far_z, turned_first, turned_last, sems):
    copies = []
    for f in range(FIELDS):
        for c in range(2):
            lanes = pl.ds(c * TILE, TILE)
            copy = pltpu.make_async_copy(v_hbm.at[f, :, lanes], pad.at[f, c, pl.ds(HALO, ROWS)], sems.at[f, c])
            copy.start()
            copies.append(copy)
    even_x, even_z = is_even("gx"), is_even("gz")
    matrix = difference_matrix()
    zeros = jnp.zeros((HALO, TILE), jnp.float32)
    for f in range(FIELDS):
        for c in range(2):
            pad[f, c, pl.ds(0, HALO)] = zeros
            pad[f, c, pl.ds(HALO + ROWS, PAD - HALO - ROWS)] = jnp.zeros((PAD - HALO - ROWS, TILE), jnp.float32)
    lane = lax.broadcasted_iota(jnp.int32, (TILE, TILE), 1)
    place = lax.broadcasted_iota(jnp.int32, (HALO, TILE), 0)
    head_weight, tail_weight = powers(place + 1), powers(HALO - place)
    for f in range(FIELDS):
        for c in range(2):
            copies[2 * f + c].wait()
        for c in range(2):
            lanes = pl.ds(c * TILE, TILE)
            head, tail = pad[f, c, pl.ds(HALO, HALO)], pad[f, c, pl.ds(ROWS, HALO)]
            head_sum = jnp.sum(head * head_weight, axis=0, keepdims=True)
            tail_sum = jnp.sum(tail * tail_weight, axis=0, keepdims=True)
            near_x[pl.ds(2 * f, 1), lanes] = jnp.where(even_x, tail_sum, head_sum)
            far_x[pl.ds(2 * f, 1), lanes] = jnp.where(even_x, head_sum, tail_sum)
            near_x[pl.ds(2 * f + 1, 1), lanes] = jnp.where(even_x, tail[HALO - 1 :], head[:1])
            far_x[pl.ds(2 * f + 1, 1), lanes] = jnp.where(even_x, head[:1], tail[HALO - 1 :])
        for b in range(BLOCKS):
            rows = pl.ds(HALO + b * TILE, TILE)
            turned = jnp.where(lane < 64, pad[f, 0, rows], pad[f, 1, rows]).T
            block = f * BLOCKS + b
            turned_first[pl.ds(block, SUB, stride=GAP)] = turned[:SUB]
            turned_last[pl.ds(block + 3, SUB, stride=GAP)] = turned[TILE - SUB :]
        if f < EARLY:
            for b in range(0, ROWS, 256):
                total = spanwise(field_rows(pad, f, b, 256), matrix)
                z_part[f, 0, pl.ds(b, 256)] = total[:, :TILE]
                z_part[f, 1, pl.ds(b, 256)] = total[:, TILE:]
    first, last = turned_first[0:EDGE], turned_last[5 * GAP + 3 : 5 * GAP + 3 + EDGE]
    near_z[...] = jnp.where(even_z, last, first)
    far_z[...] = jnp.where(even_z, first, last)


def inner_body(pad, z_part, out, swept):
    chains = [(f, c) for f in range(FIELDS) for c in (0, 1)]
    count = len(chains)

    def row(chain, k):
        f, c = chain
        return pad[f, c, pl.ds(k, SUB, stride=CHUNK)]

    def forward(step, carry):
        carry = list(carry)
        for u in range(UNROLL):
            k = step * UNROLL + u
            for n, chain in enumerate(chains):
                back2, back1, here, ahead1, y = carry[n]
                ahead2 = row(chain, k + 4)
                y = RATIO * y + (NEAR * (ahead1 - back1) + FAR * (ahead2 - back2))
                swept[n, pl.ds(pl.multiple_of(k * SUB, SUB), SUB)] = y
                carry[n] = (back1, here, ahead1, ahead2, y)
        return tuple(carry)

    zero = jnp.zeros((SUB, TILE), jnp.float32)
    start = tuple(tuple(row(chain, j) for j in range(4)) + (zero,) for chain in chains)
    lax.fori_loop(0, STEPS // UNROLL, forward, start)

    def value(n, k):
        return swept[n, pl.ds(pl.multiple_of(k * SUB, SUB), SUB)]

    carry = [zero] * count
    for k in range(WARM - 1, -1, -1):
        carry = [RATIO * carry[n] + value(n, k + WARM) for n in range(count)]
    sub = lax.broadcasted_iota(jnp.int32, (SUB, TILE), 0)
    beyond = RATIO / (1.0 - RATIO * RATIO)
    carry = [
        jnp.where(sub == SUB - 1, beyond * value(n, WARM + CHUNK - 1), pltpu.roll(carry[n], SUB - 1, 0))
        for n in range(count)
    ]

    def back(carry, k):
        carry = [RATIO * carry[n] + value(n, k + WARM) for n in range(count)]
        for n, (f, c) in enumerate(chains):
            at = pl.ds(k, SUB, stride=CHUNK)
            out[f, c, at] = carry[n] + z_part[f, c, at] if f < EARLY else carry[n]
        return carry

    def backward(step, carry):
        for u in range(UNROLL):
            carry = back(carry, CHUNK - 2 - (step * UNROLL + u))
        return tuple(carry)

    lax.fori_loop(0, CHUNK // UNROLL, backward, tuple(back(carry, CHUNK - 1)))
    matrix = difference_matrix()
    for f in range(EARLY, MIDDLE):
        for b in range(0, ROWS, 256):
            total = spanwise(field_rows(pad, f, b, 256), matrix)
            out[f, 0, pl.ds(b, 256)] += total[:, :TILE]
            out[f, 1, pl.ds(b, 256)] += total[:, TILE:]


def waits_longest():
    return lax.axis_index("gz") == 0


def first_kernel(pad, z_part, far_z_in, near_x_in, far_x_in, out, far_z, near_x, far_x, swept):
    pl.when(waits_longest())(lambda: inner_body(pad, z_part, out, swept))


def inner_kernel(pad, z_part, done, out, swept):
    pl.when(jnp.logical_not(waits_longest()))(lambda: inner_body(pad, z_part, out, swept))


def edge_kernel(pad, inner, far_z, near_z, far_x, near_x, out_hbm, work, turned_in, turned_out, sems):
    copies = []
    even_x, even_z = is_even("gx"), is_even("gz")
    matrix = difference_matrix()
    near, far = near_z[...], far_z[...]
    turned_in[0:EDGE] = jnp.where(even_z, far, near)
    turned_in[EDGE:] = jnp.where(even_z, near, far)
    l3, l2, l1 = (turned_in[n * GAP : n * GAP + TILE_ROWS] for n in range(3))
    r1, r2, r3 = (turned_in[EDGE + n * GAP : EDGE + n * GAP + TILE_ROWS] for n in range(3))
    none = jnp.zeros((TILE_ROWS, TILE), jnp.float32)
    for n, value in enumerate(
        (
            -0.75 * l1 + 0.15 * l2 - l3 * (1.0 / 60.0),
            0.15 * l1 - l2 * (1.0 / 60.0),
            l1 * (-1.0 / 60.0),
            none,
            none,
            r1 * (1.0 / 60.0),
            -0.15 * r1 + r2 * (1.0 / 60.0),
            0.75 * r1 - 0.15 * r2 + r3 * (1.0 / 60.0),
        )
    ):
        turned_out[n * GAP : n * GAP + TILE_ROWS] = value
    before, after = jnp.where(even_x, far_x[...], near_x[...]), jnp.where(even_x, near_x[...], far_x[...])
    place = lax.broadcasted_iota(jnp.int32, (HALO, TILE), 0)
    top, bottom = TAIL * powers(place), TAIL * powers(HALO - 1 - place)
    top_next, bottom_next = jnp.where(place == 0, NEXT, 0.0), jnp.where(place == HALO - 1, NEXT, 0.0)
    zeros = jnp.zeros((TILE - 2 * SUB, TILE), jnp.float32)
    lane = lax.broadcasted_iota(jnp.int32, (TILE, TILE), 1)
    for f in range(FIELDS):
        for b in range(BLOCKS):
            rows = pl.ds(b * TILE, TILE)
            columns = turned_out[pl.ds(f * BLOCKS + b, SUB, stride=GAP)]
            turned = jnp.concatenate([columns, zeros, columns]).T
            parts = [inner[f, c, rows] for c in range(2)]
            if f >= MIDDLE:
                total = spanwise(field_rows(pad, f, b * TILE, TILE), matrix)
                parts = [parts[c] + total[:, c * TILE : (c + 1) * TILE] for c in range(2)]
            work[f, 0, rows] = parts[0] + jnp.where(lane < 4, turned, 0.0)
            work[f, 1, rows] = parts[1] + jnp.where(lane < TILE - 4, 0.0, turned)
        for c in range(2):
            lanes = slice(c * TILE, (c + 1) * TILE)
            work[f, c, pl.ds(0, HALO)] += (
                top * before[2 * f : 2 * f + 1, lanes] + top_next * before[2 * f + 1 : 2 * f + 2, lanes]
            )
            work[f, c, pl.ds(ROWS - HALO, HALO)] -= (
                bottom * after[2 * f : 2 * f + 1, lanes] + bottom_next * after[2 * f + 1 : 2 * f + 2, lanes]
            )
            copy = pltpu.make_async_copy(work.at[f, c], out_hbm.at[f, :, pl.ds(c * TILE, TILE)], sems.at[f, c])
            copy.start()
            copies.append(copy)
    for copy in copies:
        copy.wait()


def vmem_spec():
    return pl.BlockSpec(memory_space=pltpu.VMEM)


def any_spec():
    return pl.BlockSpec(memory_space=pl.ANY)


def in_vmem(value):
    return pltpu.with_memory_space_constraint(value, pltpu.VMEM)


def call(kernel, outs, scratch, ins, name, aliases=None, out_specs=None):
    return pl.pallas_call(
        kernel,
        out_shape=outs,
        in_specs=[any_spec() if name == "pack" else vmem_spec() for _ in ins],
        out_specs=out_specs or (vmem_spec(),) * len(outs),
        scratch_shapes=scratch,
        input_output_aliases=aliases or {},
        compiler_params=pltpu.CompilerParams(vmem_limit_bytes=16 * MIB),
        name=name,
    )(*ins)


def on_device(velocity):
    f32 = jnp.float32
    block = pltpu.VMEM((FIELDS, 2, LONG, TILE), f32)
    x_edge, z_edge = pltpu.VMEM((2 * FIELDS, LANES), f32), pltpu.VMEM((EDGE, TILE), f32)
    turned = pltpu.VMEM((400, TILE), f32)
    sems = pltpu.SemaphoreType.DMA((FIELDS, 2))
    swept = [pltpu.VMEM((2 * FIELDS, STEPS * SUB, TILE), f32)]
    pad, z_part, near_x, far_x, near_z, far_z = call(
        pack_kernel,
        (
            pltpu.VMEM((FIELDS, 2, PAD, TILE), f32),
            pltpu.VMEM((EARLY, 2, LONG, TILE), f32),
            x_edge,
            x_edge,
            z_edge,
            z_edge,
        ),
        [turned, turned, sems],
        [pltpu.with_memory_space_constraint(velocity, pltpu.HBM)],
        "pack",
    )

    def swap(value, axis, first):
        size = lax.axis_size(axis)
        pairs = [(i % size, (i + 1) % size) for i in range(first, size, 2)]
        return lax.ppermute(value, axis, pairs + [(j, i) for i, j in pairs])

    pad, z_part = in_vmem(pad), in_vmem(z_part)
    near_z = swap(near_z, "gz", 0)
    partial, far_z, near_x, far_x = call(
        first_kernel,
        (block, z_edge, x_edge, x_edge),
        swept,
        [pad, z_part, in_vmem(far_z), in_vmem(near_x), in_vmem(far_x)],
        "first",
        {2: 1, 3: 2, 4: 3},
    )
    far_z = swap(far_z, "gz", 1)
    near_x, far_x = swap(near_x, "gx", 0), swap(far_x, "gx", 1)
    (partial,) = call(inner_kernel, (block,), swept, [pad, z_part, in_vmem(partial)], "inner", {2: 0})
    return call(
        edge_kernel,
        jax.ShapeDtypeStruct((FIELDS, ROWS, LANES), f32),
        [pltpu.VMEM((FIELDS, 2, ROWS, TILE), f32), pltpu.VMEM((2 * EDGE, TILE), f32), turned, sems],
        [pad, in_vmem(partial), far_z, near_z, far_x, near_x],
        "edges",
        None,
        any_spec(),
    )


def solution(mesh):
    return jax.shard_map(
        on_device,
        mesh=mesh,
        in_specs=(P(None, "gx", "gz"),),
        out_specs=P(None, "gx", "gz"),
        check_vma=False,
    )
```

time: 21.2 us -> 19.8 us (0.934)
  starting transfers between devices: 11.2 us -> 8.59 us
  waiting for transfers between devices: 0.01 us -> 0.92 us
  Pallas kernels: 9.86 us -> 10.1 us
    ppermute x4, starting transfers between devices: 11.2 us -> 8.59 us  [swap(): return lax.ppermute(value, axis, pairs + [(j, i) for i, j in pairs])]
    ppermute x4, waiting for transfers between devices: 0.01 us -> 0.92 us  [swap(): return lax.ppermute(value, axis, pairs + [(j, i) for i, j in pairs])]
    pallas_call x3 -> x4, Pallas kernels: 9.86 us -> 10.1 us  [call(): pl.pallas_call(kernel, out_shape=outs, in_specs=[any_spec() if name == 'p...]
  transfers between devices with their start and end apart: 4 -> 4, of which waited for: 0 -> 1; matrix products, arithmetic and copies ran while one was open for 0% -> 0% of each run, Pallas kernels for 14% -> 19%
where the time goes in v3:
time: 19.8 us; the launch traced here: 19.7 us
  Pallas kernels  10.1 us (51%)
  starting transfers between devices  8.59 us (43%)
  waiting for transfers between devices  0.92 us (5%)
    pallas_call x4, Pallas kernels, call(): pl.pallas_call(kernel, out_shape=outs, in_specs=[any_spec() if name == 'p...  10.1 us
    ppermute x4, starting transfers between devices, swap(): return lax.ppermute(value, axis, pairs + [(j, i) for i, j in pairs])  8.59 us
    ppermute x4, waiting for transfers between devices, swap(): return lax.ppermute(value, axis, pairs + [(j, i) for i, j in pairs])  0.92 us
  transfers between devices with their start and end apart: 4, of which 1 were waited for; matrix products, arithmetic and copies ran while one was open for 0% of the time, Pallas kernels for 19%

profile of v3, /device:TPU:1, one launch (start us, length us, event | category | flops | bytes accessed | tf_op | source)
XLA Modules:
  0.0 19.7 jit_solution(10565899680504622849)
XLA Ops:
  0.0 3.1 %pack.1 = (f32[4,2,1576,128]{3,2,1,0:T(8,128)S(1)}, f32[1,2,1544,128]{3,2,1,0:T(8,128)S(1)}, f32[8,256]{1,0:T(8,128)S(1)}, f32[8,256]{1,0:T(8,128)S(1)}, f32[152,128]{1,0:T(8,128)S(1)}, /*index=5*/f32[152,128]{1,0:T(8,128)S(1)}) custom-call(f32[4,1536,256]{2,1,0:T(8,128)} %v_hbm.1), custom_call_target="tpu_custom_call" | custom-call | tf_op jit(solution)/shard_map/pack/pallas_call | solution.py:259
  3.2 2.1 %collective-permute-start.1 = (f32[152,128]{1,0:T(8,128)S(1)}, f32[152,128]{1,0:T(8,128)S(1)}, u32[]{:S(2)}, u32[]{:S(2)}) collective-permute-start(f32[152,128]{1,0:T(8,128)S(1)} %get-tuple-element.22), channel_id=1, source_target_pairs={{0,1},{2,3},{4,5},{6,7},{8,9},{10,11},{12,13},{14,15},{16,17},{18,... | collective-permute-start | bytes 233480 | tf_op jit(solution)/shard_map/ppermute | solution.py:296
  5.3 3.8 %first.1 = (f32[4,2,1544,128]{3,2,1,0:T(8,128)S(1)}, f32[152,128]{1,0:T(8,128)S(1)}, f32[8,256]{1,0:T(8,128)S(1)}, f32[8,256]{1,0:T(8,128)S(1)}) custom-call(f32[4,2,1576,128]{3,2,1,0:T(8,128)S(1)} %get-tuple-element.15.pad, f32[1,2,1544,128]{3,2,1,0:T(8,128)S(1)} %get-tuple-element.16.z_part, ...), custom_call_target="tpu_custom_call", output_to_operand_aliasing={{1}: (2, {}), {2}: (3, {}), {3}: (4, {})} | custom-call | tf_op jit(solution)/shard_map/first/pallas_call | solution.py:259
  9.1 3.3 %collective-permute-start = (f32[152,128]{1,0:T(8,128)S(1)}, f32[152,128]{1,0:T(8,128)S(1)}, u32[]{:S(2)}, u32[]{:S(2)}) collective-permute-start(f32[152,128]{1,0:T(8,128)S(1)} %get-tuple-element.21), channel_id=1, source_target_pairs={{1,2},{3,4},{5,6},{7,8},{9,10},{11,12},{13,14},{15,16},{17,18},{19... | collective-permute-start | bytes 233480 | tf_op jit(solution)/shard_map/ppermute | solution.py:296
  12.4 2.4 %collective-permute-start.2 = (f32[8,256]{1,0:T(8,128)S(1)}, f32[8,256]{1,0:T(8,128)S(1)}, u32[]{:S(2)}, u32[]{:S(2)}) collective-permute-start(f32[8,256]{1,0:T(8,128)S(1)} %get-tuple-element.23), channel_id=1, source_target_pairs={{32,64},{96,128},{160,192},{224,0},{64,32},{128,96},{192,160},{0,2... | collective-permute-start | bytes 24584 | tf_op jit(solution)/shard_map/ppermute | solution.py:296
  14.8 0.7 %collective-permute-start.3 = (f32[8,256]{1,0:T(8,128)S(1)}, f32[8,256]{1,0:T(8,128)S(1)}, u32[]{:S(2)}, u32[]{:S(2)}) collective-permute-start(f32[8,256]{1,0:T(8,128)S(1)} %get-tuple-element.24), channel_id=1, source_target_pairs={{0,32},{64,96},{128,160},{192,224},{32,0},{96,64},{160,128},{224,1... | collective-permute-start | bytes 24584 | tf_op jit(solution)/shard_map/ppermute | solution.py:296
  15.5 0.9 %collective-permute-done.2.far_x = f32[8,256]{1,0:T(8,128)S(1)} collective-permute-done((f32[8,256]{1,0:T(8,128)S(1)}, f32[8,256]{1,0:T(8,128)S(1)}, u32[]{:S(2)}, u32[]{:S(2)}) %collective-permute-start.2) | collective-permute-done | bytes 8224 | tf_op jit(solution)/shard_map/ppermute | solution.py:296
  16.4 0.0 collective-permute-done.3.near_x
  16.4 0.0 collective-permute-done.1.near_z
  16.4 0.0 collective-permute-done.far_z
  16.5 3.2 %edges.1 = f32[4,1536,256]{2,1,0:T(8,128)} custom-call(f32[4,2,1576,128]{3,2,1,0:T(8,128)S(1)} %get-tuple-element.15.pad, f32[4,2,1544,128]{3,2,1,0:T(8,128)S(1)} %inner.1, f32[152,128]{1,0:T(8,128)S(1)} %collective-permute-done.far_z, f32[152,128]{1,0:T(8,128)S(1)} %collective-permute-done.1.near_z, f32[8,256]{1,0:T(8,128)S(1)} %collective-permute-done.2.far_x, ...), custom_call_target="tpu_custom_call" | custom-call | tf_op jit(solution)/shard_map/edges/pallas_call | solution.py:259
  (1 shorter events, 0.0 us)
Async XLA Ops:
  3.2 13.3 %collective-permute-start.1 = (f32[152,128]{1,0:T(8,128)S(1)}, f32[152,128]{1,0:T(8,128)S(1)}, u32[]{:S(2)}, u32[]{:S(2)}) collective-permute-start(f32[152,128]{1,0:T(8,128)S(1)} %get-tuple-element.22), channel_id=1, source_target_pairs={{0,1},{2,3},{4,5},{6,7},{8,9},{10,11},{12,13},{14,15},{16,17},{18,... | collective-permute-start | bytes 233480 | tf_op jit(solution)/shard_map/ppermute | solution.py:296
  9.1 7.4 %collective-permute-start = (f32[152,128]{1,0:T(8,128)S(1)}, f32[152,128]{1,0:T(8,128)S(1)}, u32[]{:S(2)}, u32[]{:S(2)}) collective-permute-start(f32[152,128]{1,0:T(8,128)S(1)} %get-tuple-element.21), channel_id=1, source_target_pairs={{1,2},{3,4},{5,6},{7,8},{9,10},{11,12},{13,14},{15,16},{17,18},{19... | collective-permute-start | bytes 233480 | tf_op jit(solution)/shard_map/ppermute | solution.py:296
  12.4 4.0 %collective-permute-start.2 = (f32[8,256]{1,0:T(8,128)S(1)}, f32[8,256]{1,0:T(8,128)S(1)}, u32[]{:S(2)}, u32[]{:S(2)}) collective-permute-start(f32[8,256]{1,0:T(8,128)S(1)} %get-tuple-element.23), channel_id=1, source_target_pairs={{32,64},{96,128},{160,192},{224,0},{64,32},{128,96},{192,160},{0,2... | collective-permute-start | bytes 24584 | tf_op jit(solution)/shard_map/ppermute | solution.py:296
  14.8 1.6 %collective-permute-start.3 = (f32[8,256]{1,0:T(8,128)S(1)}, f32[8,256]{1,0:T(8,128)S(1)}, u32[]{:S(2)}, u32[]{:S(2)}) collective-permute-start(f32[8,256]{1,0:T(8,128)S(1)} %get-tuple-element.24), channel_id=1, source_target_pairs={{0,32},{64,96},{128,160},{192,224},{32,0},{96,64},{160,128},{224,1... | collective-permute-start | bytes 24584 | tf_op jit(solution)/shard_map/ppermute | solution.py:296

commit v4 on v3

--- a/solution.py
+++ b/solution.py
@@ -72,7 +72,7 @@
     return lax.rem(lax.axis_index(axis), 2) == 0
 
 
-def pack_kernel(v_hbm, pad, z_part, near_x, far_x, near_z, far_z, turned_first, turned_last, sems):
+def pack_kernel(v_hbm, pad, z_part, near_x, far_x, near_x_too, far_x_too, near_z, far_z, turned_first, turned_last, sems):
     copies = []
     for f in range(FIELDS):
         for c in range(2):
@@ -114,6 +114,8 @@
                 z_part[f, 0, pl.ds(b, 256)] = total[:, :TILE]
                 z_part[f, 1, pl.ds(b, 256)] = total[:, TILE:]
     first, last = turned_first[0:EDGE], turned_last[5 * GAP + 3 : 5 * GAP + 3 + EDGE]
+    near_x_too[...] = near_x[...]
+    far_x_too[...] = far_x[...]
     near_z[...] = jnp.where(even_z, last, first)
     far_z[...] = jnp.where(even_z, first, last)
 
@@ -180,7 +182,7 @@
     return lax.axis_index("gz") == 0
 
 
-def first_kernel(pad, z_part, far_z_in, near_x_in, far_x_in, out, far_z, near_x, far_x, swept):
+def first_kernel(pad, z_part, far_z_in, near_x_in, far_x_in, far_early, near_early, out, far_z, near_x, far_x, swept):
     pl.when(waits_longest())(lambda: inner_body(pad, z_part, out, swept))
 
 
@@ -188,13 +190,9 @@
     pl.when(jnp.logical_not(waits_longest()))(lambda: inner_body(pad, z_part, out, swept))
 
 
-def edge_kernel(pad, inner, far_z, near_z, far_x, near_x, out_hbm, work, turned_in, turned_out, sems):
-    copies = []
-    even_x, even_z = is_even("gx"), is_even("gz")
-    matrix = difference_matrix()
-    near, far = near_z[...], far_z[...]
-    turned_in[0:EDGE] = jnp.where(even_z, far, near)
-    turned_in[EDGE:] = jnp.where(even_z, near, far)
+def halo_columns(left, right, turned_in, turned_out):
+    turned_in[0:EDGE] = left
+    turned_in[EDGE:] = right
     l3, l2, l1 = (turned_in[n * GAP : n * GAP + TILE_ROWS] for n in range(3))
     r1, r2, r3 = (turned_in[EDGE + n * GAP : EDGE + n * GAP + TILE_ROWS] for n in range(3))
     none = jnp.zeros((TILE_ROWS, TILE), jnp.float32)
@@ -211,36 +209,80 @@
         )
     ):
         turned_out[n * GAP : n * GAP + TILE_ROWS] = value
-    before, after = jnp.where(even_x, far_x[...], near_x[...]), jnp.where(even_x, near_x[...], far_x[...])
+
+
+def finish(sides, late, spare, pad, inner, before, after, out_hbm, work, turned_out, sems):
+    copies = []
+    matrix = difference_matrix()
     place = lax.broadcasted_iota(jnp.int32, (HALO, TILE), 0)
     top, bottom = TAIL * powers(place), TAIL * powers(HALO - 1 - place)
     top_next, bottom_next = jnp.where(place == 0, NEXT, 0.0), jnp.where(place == HALO - 1, NEXT, 0.0)
     zeros = jnp.zeros((TILE - 2 * SUB, TILE), jnp.float32)
     lane = lax.broadcasted_iota(jnp.int32, (TILE, TILE), 1)
+    half = ROWS // 2
     for f in range(FIELDS):
-        for b in range(BLOCKS):
-            rows = pl.ds(b * TILE, TILE)
-            columns = turned_out[pl.ds(f * BLOCKS + b, SUB, stride=GAP)]
-            turned = jnp.concatenate([columns, zeros, columns]).T
-            parts = [inner[f, c, rows] for c in range(2)]
-            if f >= MIDDLE:
-                total = spanwise(field_rows(pad, f, b * TILE, TILE), matrix)
-                parts = [parts[c] + total[:, c * TILE : (c + 1) * TILE] for c in range(2)]
-            work[f, 0, rows] = parts[0] + jnp.where(lane < 4, turned, 0.0)
-            work[f, 1, rows] = parts[1] + jnp.where(lane < TILE - 4, 0.0, turned)
-        for c in range(2):
-            lanes = slice(c * TILE, (c + 1) * TILE)
-            work[f, c, pl.ds(0, HALO)] += (
-                top * before[2 * f : 2 * f + 1, lanes] + top_next * before[2 * f + 1 : 2 * f + 2, lanes]
-            )
-            work[f, c, pl.ds(ROWS - HALO, HALO)] -= (
-                bottom * after[2 * f : 2 * f + 1, lanes] + bottom_next * after[2 * f + 1 : 2 * f + 2, lanes]
-            )
-            copy = pltpu.make_async_copy(work.at[f, c], out_hbm.at[f, :, pl.ds(c * TILE, TILE)], sems.at[f, c])
-            copy.start()
-            copies.append(copy)
+        for h in range(2):
+            for b in range(h * BLOCKS // 2, (h + 1) * BLOCKS // 2):
+                rows = pl.ds(b * TILE, TILE)
+                columns = turned_out[pl.ds(f * BLOCKS + b, SUB, stride=GAP)]
+                turned = jnp.concatenate([columns, zeros, columns]).T
+                parts = [inner[f, c, rows] for c in range(2)]
+                if late and f >= MIDDLE:
+                    total = spanwise(field_rows(pad, f, b * TILE, TILE), matrix)
+                    parts = [parts[c] + total[:, c * TILE : (c + 1) * TILE] for c in range(2)]
+                    if spare is not None:
+                        spare[f, 0, rows] = parts[0]
+                if 0 in sides:
+                    work[f, 0, rows] = parts[0] + jnp.where(lane < 4, turned, 0.0)
+                if 1 in sides:
+                    work[f, 1, rows] = parts[1] + jnp.where(lane < TILE - 4, 0.0, turned)
+            for c in sides:
+                lanes = slice(c * TILE, (c + 1) * TILE)
+                if h == 0:
+                    work[f, c, pl.ds(0, HALO)] += (
+                        top * before[2 * f : 2 * f + 1, lanes] + top_next * before[2 * f + 1 : 2 * f + 2, lanes]
+                    )
+                else:
+                    work[f, c, pl.ds(ROWS - HALO, HALO)] -= (
+                        bottom * after[2 * f : 2 * f + 1, lanes] + bottom_next * after[2 * f + 1 : 2 * f + 2, lanes]
+                    )
+                rows = pl.ds(h * half, half)
+                copy = pltpu.make_async_copy(
+                    work.at[f, c, rows], out_hbm.at[f, rows, pl.ds(c * TILE, TILE)], sems.at[f, c, h]
+                )
+                copy.start()
+                copies.append(copy)
     for copy in copies:
         copy.wait()
+
+
+def half_kernel(pad, inner_in, near_z, far_x, near_x, out_hbm, inner, work, turned_in, turned_out, sems):
+    def body():
+        even_x = is_even("gx")
+        before = jnp.where(even_x, far_x[...], near_x[...])
+        after = jnp.where(even_x, near_x[...], far_x[...])
+        halo_columns(jnp.zeros((EDGE, TILE), jnp.float32), near_z[...], turned_in, turned_out)
+        finish((1,), True, inner, pad, inner, before, after, out_hbm, work, turned_out, sems)
+
+    pl.when(waits_longest())(body)
+
+
+def edge_kernel(
+    pad, inner, far_z, near_z, far_x, near_x, far_early, near_early, half, out_hbm, work, turned_in, turned_out, sems
+):
+    even_x, even_z = is_even("gx"), is_even("gz")
+    far_x, near_x = far_x[...] + far_early[...], near_x[...] + near_early[...]
+    before, after = jnp.where(even_x, far_x, near_x), jnp.where(even_x, near_x, far_x)
+    left, right = jnp.where(even_z, far_z[...], near_z[...]), jnp.where(even_z, near_z[...], far_z[...])
+    halo_columns(left, right, turned_in, turned_out)
+
+    @pl.when(waits_longest())
+    def _():
+        finish((0,), False, None, pad, inner, before, after, out_hbm, work, turned_out, sems)
+
+    @pl.when(jnp.logical_not(waits_longest()))
+    def _():
+        finish((0, 1), True, None, pad, inner, before, after, out_hbm, work, turned_out, sems)
 
 
 def vmem_spec():
@@ -259,7 +301,7 @@
     return pl.pallas_call(
         kernel,
         out_shape=outs,
-        in_specs=[any_spec() if name == "pack" else vmem_spec() for _ in ins],
+        in_specs=[any_spec() if value.ndim == 3 else vmem_spec() for value in ins],
         out_specs=out_specs or (vmem_spec(),) * len(outs),
         scratch_shapes=scratch,
         input_output_aliases=aliases or {},
@@ -275,11 +317,13 @@
     turned = pltpu.VMEM((400, TILE), f32)
     sems = pltpu.SemaphoreType.DMA((FIELDS, 2))
     swept = [pltpu.VMEM((2 * FIELDS, STEPS * SUB, TILE), f32)]
-    pad, z_part, near_x, far_x, near_z, far_z = call(
+    pad, z_part, near_early, far_early, near_x, far_x, near_z, far_z = call(
         pack_kernel,
         (
             pltpu.VMEM((FIELDS, 2, PAD, TILE), f32),
             pltpu.VMEM((EARLY, 2, LONG, TILE), f32),
+            x_edge,
+            x_edge,
             x_edge,
             x_edge,
             z_edge,
@@ -290,31 +334,56 @@
         "pack",
     )
 
-    def swap(value, axis, first):
-        size = lax.axis_size(axis)
-        pairs = [(i % size, (i + 1) % size) for i in range(first, size, 2)]
-        return lax.ppermute(value, axis, pairs + [(j, i) for i, j in pairs])
+    size_x, size_z = lax.axis_size("gx"), lax.axis_size("gz")
+
+    def swap_z(value, first):
+        pairs = [(i % size_z, (i + 1) % size_z) for i in range(first, size_z, 2)]
+        return lax.ppermute(value, "gz", pairs + [(j, i) for i, j in pairs])
+
+    def swap_x(value, first, columns):
+        pairs = [
+            (i % size_x * size_z + k, (i + 1) % size_x * size_z + k) for i in range(first, size_x, 2) for k in columns
+        ]
+        return lax.ppermute(value, ("gx", "gz"), pairs + [(j, i) for i, j in pairs])
 
     pad, z_part = in_vmem(pad), in_vmem(z_part)
-    near_z = swap(near_z, "gz", 0)
+    early, others = range(1), range(1, size_z)
+    far_early, near_early = swap_x(far_early, 1, early), swap_x(near_early, 0, early)
+    near_z = swap_z(near_z, 0)
     partial, far_z, near_x, far_x = call(
         first_kernel,
         (block, z_edge, x_edge, x_edge),
         swept,
-        [pad, z_part, in_vmem(far_z), in_vmem(near_x), in_vmem(far_x)],
+        [pad, z_part, in_vmem(far_z), in_vmem(near_x), in_vmem(far_x), far_early, near_early],
         "first",
         {2: 1, 3: 2, 4: 3},
     )
-    far_z = swap(far_z, "gz", 1)
-    near_x, far_x = swap(near_x, "gx", 0), swap(far_x, "gx", 1)
+    far_z = swap_z(far_z, 1)
+    far_x, near_x = swap_x(far_x, 1, others), swap_x(near_x, 0, others)
     (partial,) = call(inner_kernel, (block,), swept, [pad, z_part, in_vmem(partial)], "inner", {2: 0})
+    work = [
+        pltpu.VMEM((FIELDS, 2, ROWS, TILE), f32),
+        pltpu.VMEM((2 * EDGE, TILE), f32),
+        turned,
+        pltpu.SemaphoreType.DMA((FIELDS, 2, 2)),
+    ]
+    whole = pltpu.HBM((FIELDS, ROWS, LANES), f32)
+    half, partial = call(
+        half_kernel,
+        (whole, block),
+        work,
+        [pad, in_vmem(partial), near_z, far_early, near_early],
+        "half",
+        {1: 1},
+        (any_spec(), vmem_spec()),
+    )
     return call(
         edge_kernel,
-        jax.ShapeDtypeStruct((FIELDS, ROWS, LANES), f32),
-        [pltpu.VMEM((FIELDS, 2, ROWS, TILE), f32), pltpu.VMEM((2 * EDGE, TILE), f32), turned, sems],
-        [pad, in_vmem(partial), far_z, near_z, far_x, near_x],
+        whole,
+        work,
+        [pad, in_vmem(partial), far_z, near_z, far_x, near_x, far_early, near_early, half],
         "edges",
-        None,
+        {8: 0},
         any_spec(),
     )
 

time: 19.8 us -> 25.6 us (1.29)
  the two profiles are of different devices: /device:TPU:1 before, /device:TPU:231 now
where the time goes in v4:
time: 25.6 us; the launch traced here: 25.5 us
  starting transfers between devices  15 us (59%)
  Pallas kernels  10.4 us (41%)
    pallas_call x5, Pallas kernels, call(): pl.pallas_call(kernel, out_shape=outs, in_specs=[any_spec() if value.ndim...  10.4 us
    ppermute x4, starting transfers between devices, swap_x(): return lax.ppermute(value, ('gx', 'gz'), pairs + [(j, i) for i, j in pairs])  7.71 us
    ppermute x2, starting transfers between devices, swap_z(): return lax.ppermute(value, 'gz', pairs + [(j, i) for i, j in pairs])  7.29 us
  transfers between devices with their start and end apart: 6, of which 0 were waited for; matrix products, arithmetic and copies ran while one was open for 0% of the time, Pallas kernels for 15%

profile of v4, /device:TPU:231, one launch (start us, length us, event | category | flops | bytes accessed | tf_op | source)
XLA Modules:
  0.0 25.5 jit_solution(4990708903440171772)
XLA Ops:
  0.0 3.2 %pack.1 = (f32[4,2,1576,128]{3,2,1,0:T(8,128)S(1)}, f32[1,2,1544,128]{3,2,1,0:T(8,128)S(1)}, f32[8,256]{1,0:T(8,128)S(1)}, f32[8,256]{1,0:T(8,128)S(1)}, f32[8,2...) custom-call(f32[4,1536,256]{2,1,0:T(8,128)} %v_hbm.1), custom_call_target="tpu_custom_call" | custom-call | tf_op jit(solution)/shard_map/pack/pallas_call | solution.py:301
  3.2 0.7 %collective-permute-start = (f32[8,256]{1,0:T(8,128)S(1)}, f32[8,256]{1,0:T(8,128)S(1)}, u32[]{:S(2)}, u32[]{:S(2)}) collective-permute-start(f32[8,256]{1,0:T(8,128)S(1)} %get-tuple-element.24), channel_id=1, source_target_pairs={{32,64},{96,128},{160,192},{224,0},{64,32},{128,96},{192,160},{0,2... | collective-permute-start | bytes 24584 | tf_op jit(solution)/shard_map/ppermute | solution.py:347
  3.8 0.7 %collective-permute-start.1 = (f32[8,256]{1,0:T(8,128)S(1)}, f32[8,256]{1,0:T(8,128)S(1)}, u32[]{:S(2)}, u32[]{:S(2)}) collective-permute-start(f32[8,256]{1,0:T(8,128)S(1)} %get-tuple-element.25), channel_id=1, source_target_pairs={{0,32},{64,96},{128,160},{192,224},{32,0},{96,64},{160,128},{224,1... | collective-permute-start | bytes 24584 | tf_op jit(solution)/shard_map/ppermute | solution.py:347
  4.5 0.6 %collective-permute-start.2 = (f32[152,128]{1,0:T(8,128)S(1)}, f32[152,128]{1,0:T(8,128)S(1)}, u32[]{:S(2)}, u32[]{:S(2)}) collective-permute-start(f32[152,128]{1,0:T(8,128)S(1)} %get-tuple-element.27), channel_id=1, source_target_pairs={{0,1},{2,3},{4,5},{6,7},{8,9},{10,11},{12,13},{14,15},{16,17},{18,... | collective-permute-start | bytes 233480 | tf_op jit(solution)/shard_map/ppermute | solution.py:341
  5.1 0.0 collective-permute-done.far_early.far_x
  5.1 0.0 collective-permute-done.1.near_early.near_x
  5.1 6.7 %collective-permute-start.3 = (f32[152,128]{1,0:T(8,128)S(1)}, f32[152,128]{1,0:T(8,128)S(1)}, u32[]{:S(2)}, u32[]{:S(2)}) collective-permute-start(f32[152,128]{1,0:T(8,128)S(1)} %get-tuple-element.29), channel_id=1, source_target_pairs={{1,2},{3,4},{5,6},{7,8},{9,10},{11,12},{13,14},{15,16},{17,18},{19... | collective-permute-start | bytes 233480 | tf_op jit(solution)/shard_map/ppermute | solution.py:341
  11.8 2.6 %collective-permute-start.4 = (f32[8,256]{1,0:T(8,128)S(1)}, f32[8,256]{1,0:T(8,128)S(1)}, u32[]{:S(2)}, u32[]{:S(2)}) collective-permute-start(f32[8,256]{1,0:T(8,128)S(1)} %get-tuple-element.30), channel_id=1, source_target_pairs={{33,65},{34,66},{35,67},{36,68},{37,69},{38,70},{39,71},{40,72},{4... | collective-permute-start | bytes 24584 | tf_op jit(solution)/shard_map/ppermute | solution.py:347
  14.4 3.8 %collective-permute-start.5 = (f32[8,256]{1,0:T(8,128)S(1)}, f32[8,256]{1,0:T(8,128)S(1)}, u32[]{:S(2)}, u32[]{:S(2)}) collective-permute-start(f32[8,256]{1,0:T(8,128)S(1)} %get-tuple-element.31), channel_id=1, source_target_pairs={{1,33},{2,34},{3,35},{4,36},{5,37},{6,38},{7,39},{8,40},{9,41},{10... | collective-permute-start | bytes 24584 | tf_op jit(solution)/shard_map/ppermute | solution.py:347
  18.2 3.8 %inner.1.inner_in = f32[4,2,1544,128]{3,2,1,0:T(8,128)S(1)} custom-call(f32[4,2,1576,128]{3,2,1,0:T(8,128)S(1)} %get-tuple-element.19.pad, f32[1,2,1544,128]{3,2,1,0:T(8,128)S(1)} %get-tuple-element.20.z_part, f32[4,2,1544,128]{3,2,1,0:T(8,128)S(1)} %get-tuple-element.26.done), custom_call_target="tpu_custom_call", output_to_operand_aliasing={{}: (2, {})} | custom-call | tf_op jit(solution)/shard_map/inner/pallas_call | solution.py:301
  22.0 0.0 collective-permute-done.2.near_z
  22.0 0.2 half.1
  22.2 0.0 collective-permute-done.4.far_x
  22.2 0.0 collective-permute-done.5.near_x
  22.2 0.0 collective-permute-done.3.far_z
  22.2 3.3 %edges.1 = f32[4,1536,256]{2,1,0:T(8,128)} custom-call(f32[4,2,1576,128]{3,2,1,0:T(8,128)S(1)} %get-tuple-element.19.pad, f32[4,2,1544,128]{3,2,1,0:T(8,128)S(1)} %get-tuple-element.28.inner, f32[152,128]{1,0:T(8,128)S(1)} %collective-permute-done.3.far_z, f32[152,128]{1,0:T(8,128)S(1)} %collective-permute-done.2.near_z, ...), custom_call_target="tpu_custom_call", output_to_operand_aliasing={{}: (8, {})} | custom-call | tf_op jit(solution)/shard_map/edges/pallas_call | solution.py:301
  (1 shorter events, 0.0 us)
Async XLA Ops:
  3.2 2.0 %collective-permute-start = (f32[8,256]{1,0:T(8,128)S(1)}, f32[8,256]{1,0:T(8,128)S(1)}, u32[]{:S(2)}, u32[]{:S(2)}) collective-permute-start(f32[8,256]{1,0:T(8,128)S(1)} %get-tuple-element.24), channel_id=1, source_target_pairs={{32,64},{96,128},{160,192},{224,0},{64,32},{128,96},{192,160},{0,2... | collective-permute-start | bytes 24584 | tf_op jit(solution)/shard_map/ppermute | solution.py:347
  3.8 1.3 %collective-permute-start.1 = (f32[8,256]{1,0:T(8,128)S(1)}, f32[8,256]{1,0:T(8,128)S(1)}, u32[]{:S(2)}, u32[]{:S(2)}) collective-permute-start(f32[8,256]{1,0:T(8,128)S(1)} %get-tuple-element.25), channel_id=1, source_target_pairs={{0,32},{64,96},{128,160},{192,224},{32,0},{96,64},{160,128},{224,1... | collective-permute-start | bytes 24584 | tf_op jit(solution)/shard_map/ppermute | solution.py:347
  4.5 17.5 %collective-permute-start.2 = (f32[152,128]{1,0:T(8,128)S(1)}, f32[152,128]{1,0:T(8,128)S(1)}, u32[]{:S(2)}, u32[]{:S(2)}) collective-permute-start(f32[152,128]{1,0:T(8,128)S(1)} %get-tuple-element.27), channel_id=1, source_target_pairs={{0,1},{2,3},{4,5},{6,7},{8,9},{10,11},{12,13},{14,15},{16,17},{18,... | collective-permute-start | bytes 233480 | tf_op jit(solution)/shard_map/ppermute | solution.py:341
  5.1 17.0 %collective-permute-start.3 = (f32[152,128]{1,0:T(8,128)S(1)}, f32[152,128]{1,0:T(8,128)S(1)}, u32[]{:S(2)}, u32[]{:S(2)}) collective-permute-start(f32[152,128]{1,0:T(8,128)S(1)} %get-tuple-element.29), channel_id=1, source_target_pairs={{1,2},{3,4},{5,6},{7,8},{9,10},{11,12},{13,14},{15,16},{17,18},{19... | collective-permute-start | bytes 233480 | tf_op jit(solution)/shard_map/ppermute | solution.py:341
  11.8 10.4 %collective-permute-start.4 = (f32[8,256]{1,0:T(8,128)S(1)}, f32[8,256]{1,0:T(8,128)S(1)}, u32[]{:S(2)}, u32[]{:S(2)}) collective-permute-start(f32[8,256]{1,0:T(8,128)S(1)} %get-tuple-element.30), channel_id=1, source_target_pairs={{33,65},{34,66},{35,67},{36,68},{37,69},{38,70},{39,71},{40,72},{4... | collective-permute-start | bytes 24584 | tf_op jit(solution)/shard_map/ppermute | solution.py:347
  14.4 7.8 %collective-permute-start.5 = (f32[8,256]{1,0:T(8,128)S(1)}, f32[8,256]{1,0:T(8,128)S(1)}, u32[]{:S(2)}, u32[]{:S(2)}) collective-permute-start(f32[8,256]{1,0:T(8,128)S(1)} %get-tuple-element.31), channel_id=1, source_target_pairs={{1,33},{2,34},{3,35},{4,36},{5,37},{6,38},{7,39},{8,40},{9,41},{10... | collective-permute-start | bytes 24584 | tf_op jit(solution)/shard_map/ppermute | solution.py:347

commit v5 on v4

--- a/solution.py
+++ b/solution.py
@@ -17,7 +17,7 @@
 STEPS = 216
 UNROLL = 8
 EARLY = 1
-MIDDLE = 2
+MIDDLE = 4
 LONG = SUB * CHUNK
 TILE = 128
 BLOCKS = ROWS // TILE
@@ -72,7 +72,7 @@
     return lax.rem(lax.axis_index(axis), 2) == 0
 
 
-def pack_kernel(v_hbm, pad, z_part, near_x, far_x, near_x_too, far_x_too, near_z, far_z, turned_first, turned_last, sems):
+def pack_kernel(v_hbm, pad, z_part, near_x, far_x, near_z, far_z, turned_first, turned_last, sems):
     copies = []
     for f in range(FIELDS):
         for c in range(2):
@@ -114,8 +114,6 @@
                 z_part[f, 0, pl.ds(b, 256)] = total[:, :TILE]
                 z_part[f, 1, pl.ds(b, 256)] = total[:, TILE:]
     first, last = turned_first[0:EDGE], turned_last[5 * GAP + 3 : 5 * GAP + 3 + EDGE]
-    near_x_too[...] = near_x[...]
-    far_x_too[...] = far_x[...]
     near_z[...] = jnp.where(even_z, last, first)
     far_z[...] = jnp.where(even_z, first, last)
 
@@ -182,7 +180,7 @@
     return lax.axis_index("gz") == 0
 
 
-def first_kernel(pad, z_part, far_z_in, near_x_in, far_x_in, far_early, near_early, out, far_z, near_x, far_x, swept):
+def first_kernel(pad, z_part, far_z_in, far_x, near_x, out, far_z, swept):
     pl.when(waits_longest())(lambda: inner_body(pad, z_part, out, swept))
 
 
@@ -211,9 +209,8 @@
         turned_out[n * GAP : n * GAP + TILE_ROWS] = value
 
 
-def finish(sides, late, spare, pad, inner, before, after, out_hbm, work, turned_out, sems):
+def finish(sides, inner, before, after, out_hbm, work, turned_out, sems):
     copies = []
-    matrix = difference_matrix()
     place = lax.broadcasted_iota(jnp.int32, (HALO, TILE), 0)
     top, bottom = TAIL * powers(place), TAIL * powers(HALO - 1 - place)
     top_next, bottom_next = jnp.where(place == 0, NEXT, 0.0), jnp.where(place == HALO - 1, NEXT, 0.0)
@@ -226,16 +223,10 @@
                 rows = pl.ds(b * TILE, TILE)
                 columns = turned_out[pl.ds(f * BLOCKS + b, SUB, stride=GAP)]
                 turned = jnp.concatenate([columns, zeros, columns]).T
-                parts = [inner[f, c, rows] for c in range(2)]
-                if late and f >= MIDDLE:
-                    total = spanwise(field_rows(pad, f, b * TILE, TILE), matrix)
-                    parts = [parts[c] + total[:, c * TILE : (c + 1) * TILE] for c in range(2)]
-                    if spare is not None:
-                        spare[f, 0, rows] = parts[0]
                 if 0 in sides:
-                    work[f, 0, rows] = parts[0] + jnp.where(lane < 4, turned, 0.0)
+                    work[f, 0, rows] = inner[f, 0, rows] + jnp.where(lane < 4, turned, 0.0)
                 if 1 in sides:
-                    work[f, 1, rows] = parts[1] + jnp.where(lane < TILE - 4, 0.0, turned)
+                    work[f, 1, rows] = inner[f, 1, rows] + jnp.where(lane < TILE - 4, 0.0, turned)
             for c in sides:
                 lanes = slice(c * TILE, (c + 1) * TILE)
                 if h == 0:
@@ -256,33 +247,31 @@
         copy.wait()
 
 
-def half_kernel(pad, inner_in, near_z, far_x, near_x, out_hbm, inner, work, turned_in, turned_out, sems):
+def half_kernel(inner, near_z, far_x, near_x, out_hbm, work, turned_in, turned_out, sems):
     def body():
         even_x = is_even("gx")
         before = jnp.where(even_x, far_x[...], near_x[...])
         after = jnp.where(even_x, near_x[...], far_x[...])
         halo_columns(jnp.zeros((EDGE, TILE), jnp.float32), near_z[...], turned_in, turned_out)
-        finish((1,), True, inner, pad, inner, before, after, out_hbm, work, turned_out, sems)
+        finish((1,), inner, before, after, out_hbm, work, turned_out, sems)
 
     pl.when(waits_longest())(body)
 
 
-def edge_kernel(
-    pad, inner, far_z, near_z, far_x, near_x, far_early, near_early, half, out_hbm, work, turned_in, turned_out, sems
-):
+def edge_kernel(inner, far_z, near_z, far_x, near_x, half, out_hbm, work, turned_in, turned_out, sems):
     even_x, even_z = is_even("gx"), is_even("gz")
-    far_x, near_x = far_x[...] + far_early[...], near_x[...] + near_early[...]
-    before, after = jnp.where(even_x, far_x, near_x), jnp.where(even_x, near_x, far_x)
+    before = jnp.where(even_x, far_x[...], near_x[...])
+    after = jnp.where(even_x, near_x[...], far_x[...])
     left, right = jnp.where(even_z, far_z[...], near_z[...]), jnp.where(even_z, near_z[...], far_z[...])
     halo_columns(left, right, turned_in, turned_out)
 
     @pl.when(waits_longest())
     def _():
-        finish((0,), False, None, pad, inner, before, after, out_hbm, work, turned_out, sems)
+        finish((0,), inner, before, after, out_hbm, work, turned_out, sems)
 
     @pl.when(jnp.logical_not(waits_longest()))
     def _():
-        finish((0, 1), True, None, pad, inner, before, after, out_hbm, work, turned_out, sems)
+        finish((0, 1), inner, before, after, out_hbm, work, turned_out, sems)
 
 
 def vmem_spec():
@@ -317,13 +306,11 @@
     turned = pltpu.VMEM((400, TILE), f32)
     sems = pltpu.SemaphoreType.DMA((FIELDS, 2))
     swept = [pltpu.VMEM((2 * FIELDS, STEPS * SUB, TILE), f32)]
-    pad, z_part, near_early, far_early, near_x, far_x, near_z, far_z = call(
+    pad, z_part, near_x, far_x, near_z, far_z = call(
         pack_kernel,
         (
             pltpu.VMEM((FIELDS, 2, PAD, TILE), f32),
             pltpu.VMEM((EARLY, 2, LONG, TILE), f32),
-            x_edge,
-            x_edge,
             x_edge,
             x_edge,
             z_edge,
@@ -334,33 +321,17 @@
         "pack",
     )
 
-    size_x, size_z = lax.axis_size("gx"), lax.axis_size("gz")
-
-    def swap_z(value, first):
-        pairs = [(i % size_z, (i + 1) % size_z) for i in range(first, size_z, 2)]
-        return lax.ppermute(value, "gz", pairs + [(j, i) for i, j in pairs])
-
-    def swap_x(value, first, columns):
-        pairs = [
-            (i % size_x * size_z + k, (i + 1) % size_x * size_z + k) for i in range(first, size_x, 2) for k in columns
-        ]
-        return lax.ppermute(value, ("gx", "gz"), pairs + [(j, i) for i, j in pairs])
+    def swap(value, axis, first):
+        size = lax.axis_size(axis)
+        pairs = [(i % size, (i + 1) % size) for i in range(first, size, 2)]
+        return lax.ppermute(value, axis, pairs + [(j, i) for i, j in pairs])
 
     pad, z_part = in_vmem(pad), in_vmem(z_part)
-    early, others = range(1), range(1, size_z)
-    far_early, near_early = swap_x(far_early, 1, early), swap_x(near_early, 0, early)
-    near_z = swap_z(near_z, 0)
-    partial, far_z, near_x, far_x = call(
-        first_kernel,
-        (block, z_edge, x_edge, x_edge),
-        swept,
-        [pad, z_part, in_vmem(far_z), in_vmem(near_x), in_vmem(far_x), far_early, near_early],
-        "first",
-        {2: 1, 3: 2, 4: 3},
-    )
-    far_z = swap_z(far_z, 1)
-    far_x, near_x = swap_x(far_x, 1, others), swap_x(near_x, 0, others)
+    near_z, far_x, near_x = swap(near_z, "gz", 0), swap(far_x, "gx", 1), swap(near_x, "gx", 0)
+    partial, far_z = call(first_kernel, (block, z_edge), swept, [pad, z_part, in_vmem(far_z), far_x, near_x], "first", {2: 1})
+    far_z = swap(far_z, "gz", 1)
     (partial,) = call(inner_kernel, (block,), swept, [pad, z_part, in_vmem(partial)], "inner", {2: 0})
+    partial = in_vmem(partial)
     work = [
         pltpu.VMEM((FIELDS, 2, ROWS, TILE), f32),
         pltpu.VMEM((2 * EDGE, TILE), f32),
@@ -368,23 +339,9 @@
         pltpu.SemaphoreType.DMA((FIELDS, 2, 2)),
     ]
     whole = pltpu.HBM((FIELDS, ROWS, LANES), f32)
-    half, partial = call(
-        half_kernel,
-        (whole, block),
-        work,
-        [pad, in_vmem(partial), near_z, far_early, near_early],
-        "half",
-        {1: 1},
-        (any_spec(), vmem_spec()),
-    )
+    half = call(half_kernel, whole, work, [partial, near_z, far_x, near_x], "half", None, any_spec())
     return call(
-        edge_kernel,
-        whole,
-        work,
-        [pad, in_vmem(partial), far_z, near_z, far_x, near_x, far_early, near_early, half],
-        "edges",
-        {8: 0},
-        any_spec(),
+        edge_kernel, whole, work, [partial, far_z, near_z, far_x, near_x, half], "edges", {5: 0}, any_spec()
     )
 
 

time: 25.6 us -> 22.5 us (0.88)
  the two profiles are of different devices: /device:TPU:231 before, /device:TPU:1 now
where the time goes in v5:
time: 22.5 us; the launch traced here: 22.1 us
  Pallas kernels  12.2 us (54%)
  starting transfers between devices  7.6 us (34%)
  waiting for transfers between devices  2.32 us (10%)
    pallas_call x5, Pallas kernels, call(): pl.pallas_call(kernel, out_shape=outs, in_specs=[any_spec() if value.ndim...  12.2 us
    ppermute x4, starting transfers between devices, swap(): return lax.ppermute(value, axis, pairs + [(j, i) for i, j in pairs])  7.6 us
    ppermute x4, waiting for transfers between devices, swap(): return lax.ppermute(value, axis, pairs + [(j, i) for i, j in pairs])  2.32 us
  transfers between devices with their start and end apart: 4, of which 1 were waited for; matrix products, arithmetic and copies ran while one was open for 0% of the time, Pallas kernels for 32%

profile of v5, /device:TPU:1, one launch (start us, length us, event | category | flops | bytes accessed | tf_op | source)
XLA Modules:
  0.0 22.1 jit_solution(7930972418345045001)
XLA Ops:
  0.0 3.1 %pack.1 = (f32[4,2,1576,128]{3,2,1,0:T(8,128)S(1)}, f32[1,2,1544,128]{3,2,1,0:T(8,128)S(1)}, f32[8,256]{1,0:T(8,128)S(1)}, f32[8,256]{1,0:T(8,128)S(1)}, f32[152,128]{1,0:T(8,128)S(1)}, /*index=5*/f32[152,128]{1,0:T(8,128)S(1)}) custom-call(f32[4,1536,256]{2,1,0:T(8,128)} %v_hbm.1), custom_call_target="tpu_custom_call" | custom-call | tf_op jit(solution)/shard_map/pack/pallas_call | solution.py:290
  3.2 2.8 %collective-permute-start = (f32[8,256]{1,0:T(8,128)S(1)}, f32[8,256]{1,0:T(8,128)S(1)}, u32[]{:S(2)}, u32[]{:S(2)}) collective-permute-start(f32[8,256]{1,0:T(8,128)S(1)} %get-tuple-element.16), channel_id=1, source_target_pairs={{32,64},{96,128},{160,192},{224,0},{64,32},{128,96},{192,160},{0,2... | collective-permute-start | bytes 24584 | tf_op jit(solution)/shard_map/ppermute | solution.py:327
  5.9 1.3 %collective-permute-start.1 = (f32[8,256]{1,0:T(8,128)S(1)}, f32[8,256]{1,0:T(8,128)S(1)}, u32[]{:S(2)}, u32[]{:S(2)}) collective-permute-start(f32[8,256]{1,0:T(8,128)S(1)} %get-tuple-element.17), channel_id=1, source_target_pairs={{0,32},{64,96},{128,160},{192,224},{32,0},{96,64},{160,128},{224,1... | collective-permute-start | bytes 24584 | tf_op jit(solution)/shard_map/ppermute | solution.py:327
  7.2 1.2 %collective-permute-start.3 = (f32[152,128]{1,0:T(8,128)S(1)}, f32[152,128]{1,0:T(8,128)S(1)}, u32[]{:S(2)}, u32[]{:S(2)}) collective-permute-start(f32[152,128]{1,0:T(8,128)S(1)} %get-tuple-element.20), channel_id=1, source_target_pairs={{0,1},{2,3},{4,5},{6,7},{8,9},{10,11},{12,13},{14,15},{16,17},{18,... | collective-permute-start | bytes 233480 | tf_op jit(solution)/shard_map/ppermute | solution.py:327
  8.4 0.0 collective-permute-done.far_x
  8.4 0.0 collective-permute-done.1.near_x
  8.4 5.0 %first.1 = (f32[4,2,1544,128]{3,2,1,0:T(8,128)S(1)}, f32[152,128]{1,0:T(8,128)S(1)}) custom-call(f32[4,2,1576,128]{3,2,1,0:T(8,128)S(1)} %get-tuple-element.13.pad, f32[1,2,1544,128]{3,2,1,0:T(8,128)S(1)} %get-tuple-element.14.z_part, f32[152,128]{1,0:T(8,128)S(1)} %get-tuple-element.15.far_z_in, ...), custom_call_target="tpu_custom_call", output_to_operand_aliasing={{1}: (2, {})} | custom-call | tf_op jit(solution)/shard_map/first/pallas_call | solution.py:290
  13.5 2.3 %collective-permute-start.2 = (f32[152,128]{1,0:T(8,128)S(1)}, f32[152,128]{1,0:T(8,128)S(1)}, u32[]{:S(2)}, u32[]{:S(2)}) collective-permute-start(f32[152,128]{1,0:T(8,128)S(1)} %get-tuple-element.19), channel_id=1, source_target_pairs={{1,2},{3,4},{5,6},{7,8},{9,10},{11,12},{13,14},{15,16},{17,18},{19... | collective-permute-start | bytes 233480 | tf_op jit(solution)/shard_map/ppermute | solution.py:327
  15.8 0.0 collective-permute-done.3.near_z
  15.8 2.0 %half.1 = f32[4,1536,256]{2,1,0:T(8,128)} custom-call(f32[4,2,1544,128]{3,2,1,0:T(8,128)S(1)} %inner.1, f32[152,128]{1,0:T(8,128)S(1)} %collective-permute-done.3.near_z, f32[8,256]{1,0:T(8,128)S(1)} %collective-permute-done.far_x, f32[8,256]{1,0:T(8,128)S(1)} %collective-permute-done.1.near_x), custom_call_target="tpu_custom_call" | custom-call | tf_op jit(solution)/shard_map/half/pallas_call | solution.py:290
  17.8 2.3 %collective-permute-done.2.far_z = f32[152,128]{1,0:T(8,128)S(1)} collective-permute-done((f32[152,128]{1,0:T(8,128)S(1)}, f32[152,128]{1,0:T(8,128)S(1)}, u32[]{:S(2)}, u32[]{:S(2)}) %collective-permute-start.2) | collective-permute-done | bytes 77856 | tf_op jit(solution)/shard_map/ppermute | solution.py:327
  20.1 2.0 %edges.1 = f32[4,1536,256]{2,1,0:T(8,128)} custom-call(f32[4,2,1544,128]{3,2,1,0:T(8,128)S(1)} %inner.1, f32[152,128]{1,0:T(8,128)S(1)} %collective-permute-done.2.far_z, f32[152,128]{1,0:T(8,128)S(1)} %collective-permute-done.3.near_z, f32[8,256]{1,0:T(8,128)S(1)} %collective-permute-done.far_x, ...), custom_call_target="tpu_custom_call", output_to_operand_aliasing={{}: (5, {})} | custom-call | tf_op jit(solution)/shard_map/edges/pallas_call | solution.py:290
  (1 shorter events, 0.0 us)
Async XLA Ops:
  3.2 5.3 %collective-permute-start = (f32[8,256]{1,0:T(8,128)S(1)}, f32[8,256]{1,0:T(8,128)S(1)}, u32[]{:S(2)}, u32[]{:S(2)}) collective-permute-start(f32[8,256]{1,0:T(8,128)S(1)} %get-tuple-element.16), channel_id=1, source_target_pairs={{32,64},{96,128},{160,192},{224,0},{64,32},{128,96},{192,160},{0,2... | collective-permute-start | bytes 24584 | tf_op jit(solution)/shard_map/ppermute | solution.py:327
  5.9 2.5 %collective-permute-start.1 = (f32[8,256]{1,0:T(8,128)S(1)}, f32[8,256]{1,0:T(8,128)S(1)}, u32[]{:S(2)}, u32[]{:S(2)}) collective-permute-start(f32[8,256]{1,0:T(8,128)S(1)} %get-tuple-element.17), channel_id=1, source_target_pairs={{0,32},{64,96},{128,160},{192,224},{32,0},{96,64},{160,128},{224,1... | collective-permute-start | bytes 24584 | tf_op jit(solution)/shard_map/ppermute | solution.py:327
  7.2 8.6 %collective-permute-start.3 = (f32[152,128]{1,0:T(8,128)S(1)}, f32[152,128]{1,0:T(8,128)S(1)}, u32[]{:S(2)}, u32[]{:S(2)}) collective-permute-start(f32[152,128]{1,0:T(8,128)S(1)} %get-tuple-element.20), channel_id=1, source_target_pairs={{0,1},{2,3},{4,5},{6,7},{8,9},{10,11},{12,13},{14,15},{16,17},{18,... | collective-permute-start | bytes 233480 | tf_op jit(solution)/shard_map/ppermute | solution.py:327
  13.5 6.7 %collective-permute-start.2 = (f32[152,128]{1,0:T(8,128)S(1)}, f32[152,128]{1,0:T(8,128)S(1)}, u32[]{:S(2)}, u32[]{:S(2)}) collective-permute-start(f32[152,128]{1,0:T(8,128)S(1)} %get-tuple-element.19), channel_id=1, source_target_pairs={{1,2},{3,4},{5,6},{7,8},{9,10},{11,12},{13,14},{15,16},{17,18},{19... | collective-permute-start | bytes 233480 | tf_op jit(solution)/shard_map/ppermute | solution.py:327

commit v6 on v3

--- a/solution.py
+++ b/solution.py
@@ -31,6 +31,7 @@
 
 GAP = TILE_ROWS + 1
 EDGE = 152
+FAR_EDGE = 160
 SCALE = 1.0 / (KAPPA * (1.0 - RATIO * RATIO))
 TAIL = SCALE * (7.0 / 9.0 * (RATIO - 1.0 / RATIO) + 1.0 / 36.0 * (RATIO**2 - RATIO**-2))
 NEXT = -1.0 / 12.0
@@ -115,7 +116,8 @@
                 z_part[f, 1, pl.ds(b, 256)] = total[:, TILE:]
     first, last = turned_first[0:EDGE], turned_last[5 * GAP + 3 : 5 * GAP + 3 + EDGE]
     near_z[...] = jnp.where(even_z, last, first)
-    far_z[...] = jnp.where(even_z, first, last)
+    far_z[0:EDGE] = jnp.where(even_z, first, last)
+    far_z[EDGE:] = jnp.zeros((FAR_EDGE - EDGE, TILE), jnp.float32)
 
 
 def inner_body(pad, z_part, out, swept):
@@ -176,23 +178,27 @@
             out[f, 1, pl.ds(b, 256)] += total[:, TILE:]
 
 
-def waits_longest():
-    return lax.axis_index("gz") == 0
-
-
-def first_kernel(pad, z_part, far_z_in, near_x_in, far_x_in, out, far_z, near_x, far_x, swept):
-    pl.when(waits_longest())(lambda: inner_body(pad, z_part, out, swept))
+def place_z():
+    return lax.axis_index("gz")
+
+
+def first_kernel(pad, z_part, far_z_in, out, far_z, swept):
+    pl.when(place_z() == 0)(lambda: inner_body(pad, z_part, out, swept))
+
+
+def second_kernel(pad, z_part, done, near_z_in, near_x_in, far_x_in, out, near_z, near_x, far_x, swept):
+    pl.when(place_z() == 1)(lambda: inner_body(pad, z_part, out, swept))
 
 
 def inner_kernel(pad, z_part, done, out, swept):
-    pl.when(jnp.logical_not(waits_longest()))(lambda: inner_body(pad, z_part, out, swept))
+    pl.when(place_z() > 1)(lambda: inner_body(pad, z_part, out, swept))
 
 
 def edge_kernel(pad, inner, far_z, near_z, far_x, near_x, out_hbm, work, turned_in, turned_out, sems):
     copies = []
     even_x, even_z = is_even("gx"), is_even("gz")
     matrix = difference_matrix()
-    near, far = near_z[...], far_z[...]
+    near, far = near_z[...], far_z[0:EDGE]
     turned_in[0:EDGE] = jnp.where(even_z, far, near)
     turned_in[EDGE:] = jnp.where(even_z, near, far)
     l3, l2, l1 = (turned_in[n * GAP : n * GAP + TILE_ROWS] for n in range(3))
@@ -272,6 +278,7 @@
     f32 = jnp.float32
     block = pltpu.VMEM((FIELDS, 2, LONG, TILE), f32)
     x_edge, z_edge = pltpu.VMEM((2 * FIELDS, LANES), f32), pltpu.VMEM((EDGE, TILE), f32)
+    far_edge = pltpu.VMEM((FAR_EDGE, TILE), f32)
     turned = pltpu.VMEM((400, TILE), f32)
     sems = pltpu.SemaphoreType.DMA((FIELDS, 2))
     swept = [pltpu.VMEM((2 * FIELDS, STEPS * SUB, TILE), f32)]
@@ -283,7 +290,7 @@
             x_edge,
             x_edge,
             z_edge,
-            z_edge,
+            far_edge,
         ),
         [turned, turned, sems],
         [pltpu.with_memory_space_constraint(velocity, pltpu.HBM)],
@@ -296,16 +303,17 @@
         return lax.ppermute(value, axis, pairs + [(j, i) for i, j in pairs])
 
     pad, z_part = in_vmem(pad), in_vmem(z_part)
-    near_z = swap(near_z, "gz", 0)
-    partial, far_z, near_x, far_x = call(
-        first_kernel,
+    partial, far_z = call(first_kernel, (block, far_edge), swept, [pad, z_part, in_vmem(far_z)], "first", {2: 1})
+    far_z = swap(far_z, "gz", 1)
+    partial, near_z, near_x, far_x = call(
+        second_kernel,
         (block, z_edge, x_edge, x_edge),
         swept,
-        [pad, z_part, in_vmem(far_z), in_vmem(near_x), in_vmem(far_x)],
-        "first",
-        {2: 1, 3: 2, 4: 3},
-    )
-    far_z = swap(far_z, "gz", 1)
+        [pad, z_part, in_vmem(partial), in_vmem(near_z), in_vmem(near_x), in_vmem(far_x)],
+        "second",
+        {2: 0, 3: 1, 4: 2, 5: 3},
+    )
+    near_z = swap(near_z, "gz", 0)
     near_x, far_x = swap(near_x, "gx", 0), swap(far_x, "gx", 1)
     (partial,) = call(inner_kernel, (block,), swept, [pad, z_part, in_vmem(partial)], "inner", {2: 0})
     return call(

time: 19.8 us -> 19.4 us (0.980); the launches traced: 19.7 us -> 19.1 us
  starting transfers between devices: 8.59 us -> 8.06 us
    ppermute x4, starting transfers between devices: 8.59 us -> 8.06 us  [swap(): return lax.ppermute(value, axis, pairs + [(j, i) for i, j in pairs])]
    pallas_call x4 -> x5, Pallas kernels: 10.1 us -> 10.2 us  [call(): pl.pallas_call(kernel, out_shape=outs, in_specs=[any_spec() if name == 'p...]
  transfers between devices with their start and end apart: 4 -> 4, of which waited for: 1 -> 2; matrix products, arithmetic and copies ran while one was open for 0% -> 0% of each run, Pallas kernels for 19% -> 0%
where the time goes in v6:
time: 19.4 us; the launch traced here: 19.1 us
  Pallas kernels  10.2 us (53%)
  starting transfers between devices  8.06 us (42%)
  waiting for transfers between devices  0.83 us (4%)
    pallas_call x5, Pallas kernels, call(): pl.pallas_call(kernel, out_shape=outs, in_specs=[any_spec() if name == 'p...  10.2 us
    ppermute x4, starting transfers between devices, swap(): return lax.ppermute(value, axis, pairs + [(j, i) for i, j in pairs])  8.06 us
    ppermute x4, waiting for transfers between devices, swap(): return lax.ppermute(value, axis, pairs + [(j, i) for i, j in pairs])  0.83 us
  transfers between devices with their start and end apart: 4, of which 2 were waited for; matrix products, arithmetic and copies ran while one was open for 0% of the time, Pallas kernels for 0%

profile of v6, /device:TPU:1, one launch (start us, length us, event | category | flops | bytes accessed | tf_op | source)
XLA Modules:
  0.0 19.1 jit_solution(17744156006183321385)
XLA Ops:
  0.0 3.1 %pack.1 = (f32[4,2,1576,128]{3,2,1,0:T(8,128)S(1)}, f32[1,2,1544,128]{3,2,1,0:T(8,128)S(1)}, f32[8,256]{1,0:T(8,128)S(1)}, f32[8,256]{1,0:T(8,128)S(1)}, f32[152,128]{1,0:T(8,128)S(1)}, /*index=5*/f32[160,128]{1,0:T(8,128)S(1)}) custom-call(f32[4,1536,256]{2,1,0:T(8,128)} %v_hbm.1), custom_call_target="tpu_custom_call" | custom-call | tf_op jit(solution)/shard_map/pack/pallas_call | solution.py:265
  3.2 3.8 %first.1 = (f32[4,2,1544,128]{3,2,1,0:T(8,128)S(1)}, f32[160,128]{1,0:T(8,128)S(1)}) custom-call(f32[4,2,1576,128]{3,2,1,0:T(8,128)S(1)} %get-tuple-element.17.pad, f32[1,2,1544,128]{3,2,1,0:T(8,128)S(1)} %get-tuple-element.18.z_part, f32[160,128]{1,0:T(8,128)S(1)} %get-tuple-element.19.far_z_in), custom_call_target="tpu_custom_call", output_to_operand_aliasing={{1}: (2, {})} | custom-call | tf_op jit(solution)/shard_map/first/pallas_call | solution.py:265
  6.9 4.9 %collective-permute-start = (f32[160,128]{1,0:T(8,128)S(1)}, f32[160,128]{1,0:T(8,128)S(1)}, u32[]{:S(2)}, u32[]{:S(2)}) collective-permute-start(f32[160,128]{1,0:T(8,128)S(1)} %get-tuple-element.25), channel_id=1, source_target_pairs={{1,2},{3,4},{5,6},{7,8},{9,10},{11,12},{13,14},{15,16},{17,18},{19... | collective-permute-start | bytes 245768 | tf_op jit(solution)/shard_map/ppermute | solution.py:303
  11.9 0.0 collective-permute-start.1
  11.9 2.1 %collective-permute-start.2 = (f32[8,256]{1,0:T(8,128)S(1)}, f32[8,256]{1,0:T(8,128)S(1)}, u32[]{:S(2)}, u32[]{:S(2)}) collective-permute-start(f32[8,256]{1,0:T(8,128)S(1)} %get-tuple-element.27), channel_id=1, source_target_pairs={{32,64},{96,128},{160,192},{224,0},{64,32},{128,96},{192,160},{0,2... | collective-permute-start | bytes 24584 | tf_op jit(solution)/shard_map/ppermute | solution.py:303
  14.0 1.0 %collective-permute-start.3 = (f32[8,256]{1,0:T(8,128)S(1)}, f32[8,256]{1,0:T(8,128)S(1)}, u32[]{:S(2)}, u32[]{:S(2)}) collective-permute-start(f32[8,256]{1,0:T(8,128)S(1)} %get-tuple-element.28), channel_id=1, source_target_pairs={{0,32},{64,96},{128,160},{192,224},{32,0},{96,64},{160,128},{224,1... | collective-permute-start | bytes 24584 | tf_op jit(solution)/shard_map/ppermute | solution.py:303
  15.0 0.3 %collective-permute-done.2.far_x = f32[8,256]{1,0:T(8,128)S(1)} collective-permute-done((f32[8,256]{1,0:T(8,128)S(1)}, f32[8,256]{1,0:T(8,128)S(1)}, u32[]{:S(2)}, u32[]{:S(2)}) %collective-permute-start.2) | collective-permute-done | bytes 8224 | tf_op jit(solution)/shard_map/ppermute | solution.py:303
  15.3 0.5 %collective-permute-done.3.near_x = f32[8,256]{1,0:T(8,128)S(1)} collective-permute-done((f32[8,256]{1,0:T(8,128)S(1)}, f32[8,256]{1,0:T(8,128)S(1)}, u32[]{:S(2)}, u32[]{:S(2)}) %collective-permute-start.3) | collective-permute-done | bytes 8224 | tf_op jit(solution)/shard_map/ppermute | solution.py:303
  15.8 0.0 collective-permute-done.1.near_z
  15.8 0.0 collective-permute-done.far_z
  15.8 3.2 %edges.1 = f32[4,1536,256]{2,1,0:T(8,128)} custom-call(f32[4,2,1576,128]{3,2,1,0:T(8,128)S(1)} %get-tuple-element.17.pad, f32[4,2,1544,128]{3,2,1,0:T(8,128)S(1)} %inner.1, f32[160,128]{1,0:T(8,128)S(1)} %collective-permute-done.far_z, f32[152,128]{1,0:T(8,128)S(1)} %collective-permute-done.1.near_z, f32[8,256]{1,0:T(8,128)S(1)} %collective-permute-done.2.far_x, ...), custom_call_target="tpu_custom_call" | custom-call | tf_op jit(solution)/shard_map/edges/pallas_call | solution.py:265
  (2 shorter events, 0.0 us)
Async XLA Ops:
  6.9 8.9 %collective-permute-start = (f32[160,128]{1,0:T(8,128)S(1)}, f32[160,128]{1,0:T(8,128)S(1)}, u32[]{:S(2)}, u32[]{:S(2)}) collective-permute-start(f32[160,128]{1,0:T(8,128)S(1)} %get-tuple-element.25), channel_id=1, source_target_pairs={{1,2},{3,4},{5,6},{7,8},{9,10},{11,12},{13,14},{15,16},{17,18},{19... | collective-permute-start | bytes 245768 | tf_op jit(solution)/shard_map/ppermute | solution.py:303
  11.9 4.0 %collective-permute-start.1 = (f32[152,128]{1,0:T(8,128)S(1)}, f32[152,128]{1,0:T(8,128)S(1)}, u32[]{:S(2)}, u32[]{:S(2)}) collective-permute-start(f32[152,128]{1,0:T(8,128)S(1)} %get-tuple-element.26), channel_id=1, source_target_pairs={{0,1},{2,3},{4,5},{6,7},{8,9},{10,11},{12,13},{14,15},{16,17},{18,... | collective-permute-start | bytes 233480 | tf_op jit(solution)/shard_map/ppermute | solution.py:303
  11.9 3.5 %collective-permute-start.2 = (f32[8,256]{1,0:T(8,128)S(1)}, f32[8,256]{1,0:T(8,128)S(1)}, u32[]{:S(2)}, u32[]{:S(2)}) collective-permute-start(f32[8,256]{1,0:T(8,128)S(1)} %get-tuple-element.27), channel_id=1, source_target_pairs={{32,64},{96,128},{160,192},{224,0},{64,32},{128,96},{192,160},{0,2... | collective-permute-start | bytes 24584 | tf_op jit(solution)/shard_map/ppermute | solution.py:303
  14.0 1.8 %collective-permute-start.3 = (f32[8,256]{1,0:T(8,128)S(1)}, f32[8,256]{1,0:T(8,128)S(1)}, u32[]{:S(2)}, u32[]{:S(2)}) collective-permute-start(f32[8,256]{1,0:T(8,128)S(1)} %get-tuple-element.28), channel_id=1, source_target_pairs={{0,32},{64,96},{128,160},{192,224},{32,0},{96,64},{160,128},{224,1... | collective-permute-start | bytes 24584 | tf_op jit(solution)/shard_map/ppermute | solution.py:303

commit v7 on v5

--- a/solution.py
+++ b/solution.py
@@ -17,7 +17,7 @@
 STEPS = 216
 UNROLL = 8
 EARLY = 1
-MIDDLE = 4
+MIDDLE = 2
 LONG = SUB * CHUNK
 TILE = 128
 BLOCKS = ROWS // TILE
@@ -31,6 +31,7 @@
 
 GAP = TILE_ROWS + 1
 EDGE = 152
+FAR_EDGE = 160
 SCALE = 1.0 / (KAPPA * (1.0 - RATIO * RATIO))
 TAIL = SCALE * (7.0 / 9.0 * (RATIO - 1.0 / RATIO) + 1.0 / 36.0 * (RATIO**2 - RATIO**-2))
 NEXT = -1.0 / 12.0
@@ -115,7 +116,8 @@
                 z_part[f, 1, pl.ds(b, 256)] = total[:, TILE:]
     first, last = turned_first[0:EDGE], turned_last[5 * GAP + 3 : 5 * GAP + 3 + EDGE]
     near_z[...] = jnp.where(even_z, last, first)
-    far_z[...] = jnp.where(even_z, first, last)
+    far_z[0:EDGE] = jnp.where(even_z, first, last)
+    far_z[EDGE:] = jnp.zeros((FAR_EDGE - EDGE, TILE), jnp.float32)
 
 
 def inner_body(pad, z_part, out, swept):
@@ -168,24 +170,36 @@
         return tuple(carry)
 
     lax.fori_loop(0, CHUNK // UNROLL, backward, tuple(back(carry, CHUNK - 1)))
+    add_spanwise(pad, out, range(EARLY, MIDDLE))
+
+
+def add_spanwise(pad, out, fields):
     matrix = difference_matrix()
-    for f in range(EARLY, MIDDLE):
+    for f in fields:
         for b in range(0, ROWS, 256):
             total = spanwise(field_rows(pad, f, b, 256), matrix)
             out[f, 0, pl.ds(b, 256)] += total[:, :TILE]
             out[f, 1, pl.ds(b, 256)] += total[:, TILE:]
 
 
-def waits_longest():
-    return lax.axis_index("gz") == 0
-
-
-def first_kernel(pad, z_part, far_z_in, far_x, near_x, out, far_z, swept):
-    pl.when(waits_longest())(lambda: inner_body(pad, z_part, out, swept))
+def place_z():
+    return lax.axis_index("gz")
+
+
+def first_kernel(pad, z_part, far_z_in, out, far_z, swept):
+    pl.when(place_z() == 0)(lambda: inner_body(pad, z_part, out, swept))
+
+
+def second_kernel(pad, z_part, done, near_z_in, near_x_in, far_x_in, out, near_z, near_x, far_x, swept):
+    @pl.when(place_z() == 1)
+    def _():
+        inner_body(pad, z_part, out, swept)
+        add_spanwise(pad, out, range(MIDDLE, FIELDS))
 
 
 def inner_kernel(pad, z_part, done, out, swept):
-    pl.when(jnp.logical_not(waits_longest()))(lambda: inner_body(pad, z_part, out, swept))
+    pl.when(place_z() > 1)(lambda: inner_body(pad, z_part, out, swept))
+    pl.when(place_z() == 0)(lambda: add_spanwise(pad, out, range(MIDDLE, FIELDS)))
 
 
 def halo_columns(left, right, turned_in, turned_out):
@@ -209,13 +223,15 @@
         turned_out[n * GAP : n * GAP + TILE_ROWS] = value
 
 
-def finish(sides, inner, before, after, out_hbm, work, turned_out, sems):
+def finish(whole, rims, middles, late, pad, inner, before, after, out_hbm, work, turned_out, sems):
     copies = []
+    matrix = difference_matrix()
     place = lax.broadcasted_iota(jnp.int32, (HALO, TILE), 0)
     top, bottom = TAIL * powers(place), TAIL * powers(HALO - 1 - place)
     top_next, bottom_next = jnp.where(place == 0, NEXT, 0.0), jnp.where(place == HALO - 1, NEXT, 0.0)
     zeros = jnp.zeros((TILE - 2 * SUB, TILE), jnp.float32)
     lane = lax.broadcasted_iota(jnp.int32, (TILE, TILE), 1)
+    own = (lane < 4, lane >= TILE - 4)
     half = ROWS // 2
     for f in range(FIELDS):
         for h in range(2):
@@ -223,21 +239,30 @@
                 rows = pl.ds(b * TILE, TILE)
                 columns = turned_out[pl.ds(f * BLOCKS + b, SUB, stride=GAP)]
                 turned = jnp.concatenate([columns, zeros, columns]).T
-                if 0 in sides:
-                    work[f, 0, rows] = inner[f, 0, rows] + jnp.where(lane < 4, turned, 0.0)
-                if 1 in sides:
-                    work[f, 1, rows] = inner[f, 1, rows] + jnp.where(lane < TILE - 4, 0.0, turned)
-            for c in sides:
+                if late and f >= MIDDLE:
+                    total = spanwise(field_rows(pad, f, b * TILE, TILE), matrix)
+                for c in whole + middles + (rims if b in (0, BLOCKS - 1) else ()):
+                    value = inner[f, c, rows]
+                    if late and f >= MIDDLE:
+                        value = value + total[:, c * TILE : (c + 1) * TILE]
+                    work[f, c, rows] = value + jnp.where(own[c], turned, 0.0)
+            outer = pl.ds(0, HALO) if h == 0 else pl.ds(ROWS - HALO, HALO)
+            for c in whole + rims:
                 lanes = slice(c * TILE, (c + 1) * TILE)
                 if h == 0:
-                    work[f, c, pl.ds(0, HALO)] += (
+                    work[f, c, outer] += (
                         top * before[2 * f : 2 * f + 1, lanes] + top_next * before[2 * f + 1 : 2 * f + 2, lanes]
                     )
                 else:
-                    work[f, c, pl.ds(ROWS - HALO, HALO)] -= (
+                    work[f, c, outer] -= (
                         bottom * after[2 * f : 2 * f + 1, lanes] + bottom_next * after[2 * f + 1 : 2 * f + 2, lanes]
                     )
-                rows = pl.ds(h * half, half)
+            for c in whole + rims + middles:
+                rows = outer
+                if c in whole:
+                    rows = pl.ds(h * half, half)
+                elif c in middles:
+                    rows = pl.ds(HALO if h == 0 else half, half - HALO)
                 copy = pltpu.make_async_copy(
                     work.at[f, c, rows], out_hbm.at[f, rows, pl.ds(c * TILE, TILE)], sems.at[f, c, h]
                 )
@@ -247,31 +272,23 @@
         copy.wait()
 
 
-def half_kernel(inner, near_z, far_x, near_x, out_hbm, work, turned_in, turned_out, sems):
-    def body():
-        even_x = is_even("gx")
-        before = jnp.where(even_x, far_x[...], near_x[...])
-        after = jnp.where(even_x, near_x[...], far_x[...])
-        halo_columns(jnp.zeros((EDGE, TILE), jnp.float32), near_z[...], turned_in, turned_out)
-        finish((1,), inner, before, after, out_hbm, work, turned_out, sems)
-
-    pl.when(waits_longest())(body)
-
-
-def edge_kernel(inner, far_z, near_z, far_x, near_x, half, out_hbm, work, turned_in, turned_out, sems):
+def half_kernel(pad, inner, far_z, out_hbm, work, turned_in, turned_out, sems):
+    @pl.when(place_z() == 1)
+    def _():
+        halo_columns(jnp.zeros((EDGE, TILE), jnp.float32), far_z[0:EDGE], turned_in, turned_out)
+        finish((), (), (1,), False, pad, inner, None, None, out_hbm, work, turned_out, sems)
+
+
+def edge_kernel(pad, inner, far_z, near_z, far_x, near_x, half, out_hbm, work, turned_in, turned_out, sems):
     even_x, even_z = is_even("gx"), is_even("gz")
     before = jnp.where(even_x, far_x[...], near_x[...])
     after = jnp.where(even_x, near_x[...], far_x[...])
-    left, right = jnp.where(even_z, far_z[...], near_z[...]), jnp.where(even_z, near_z[...], far_z[...])
-    halo_columns(left, right, turned_in, turned_out)
-
-    @pl.when(waits_longest())
-    def _():
-        finish((0,), inner, before, after, out_hbm, work, turned_out, sems)
-
-    @pl.when(jnp.logical_not(waits_longest()))
-    def _():
-        finish((0, 1), inner, before, after, out_hbm, work, turned_out, sems)
+    near, far = near_z[...], far_z[0:EDGE]
+    halo_columns(jnp.where(even_z, far, near), jnp.where(even_z, near, far), turned_in, turned_out)
+    rest = (pad, inner, before, after, out_hbm, work, turned_out, sems)
+    pl.when(place_z() == 0)(lambda: finish((0, 1), (), (), False, *rest))
+    pl.when(place_z() == 1)(lambda: finish((0,), (1,), (), False, *rest))
+    pl.when(place_z() > 1)(lambda: finish((0, 1), (), (), True, *rest))
 
 
 def vmem_spec():
@@ -303,8 +320,8 @@
     f32 = jnp.float32
     block = pltpu.VMEM((FIELDS, 2, LONG, TILE), f32)
     x_edge, z_edge = pltpu.VMEM((2 * FIELDS, LANES), f32), pltpu.VMEM((EDGE, TILE), f32)
+    far_edge = pltpu.VMEM((FAR_EDGE, TILE), f32)
     turned = pltpu.VMEM((400, TILE), f32)
-    sems = pltpu.SemaphoreType.DMA((FIELDS, 2))
     swept = [pltpu.VMEM((2 * FIELDS, STEPS * SUB, TILE), f32)]
     pad, z_part, near_x, far_x, near_z, far_z = call(
         pack_kernel,
@@ -314,9 +331,9 @@
             x_edge,
             x_edge,
             z_edge,
-            z_edge,
+            far_edge,
         ),
-        [turned, turned, sems],
+        [turned, turned, pltpu.SemaphoreType.DMA((FIELDS, 2))],
         [pltpu.with_memory_space_constraint(velocity, pltpu.HBM)],
         "pack",
     )
@@ -327,9 +344,18 @@
         return lax.ppermute(value, axis, pairs + [(j, i) for i, j in pairs])
 
     pad, z_part = in_vmem(pad), in_vmem(z_part)
-    near_z, far_x, near_x = swap(near_z, "gz", 0), swap(far_x, "gx", 1), swap(near_x, "gx", 0)
-    partial, far_z = call(first_kernel, (block, z_edge), swept, [pad, z_part, in_vmem(far_z), far_x, near_x], "first", {2: 1})
+    partial, far_z = call(first_kernel, (block, far_edge), swept, [pad, z_part, in_vmem(far_z)], "first", {2: 1})
     far_z = swap(far_z, "gz", 1)
+    partial, near_z, near_x, far_x = call(
+        second_kernel,
+        (block, z_edge, x_edge, x_edge),
+        swept,
+        [pad, z_part, in_vmem(partial), in_vmem(near_z), in_vmem(near_x), in_vmem(far_x)],
+        "second",
+        {2: 0, 3: 1, 4: 2, 5: 3},
+    )
+    near_z = swap(near_z, "gz", 0)
+    near_x, far_x = swap(near_x, "gx", 0), swap(far_x, "gx", 1)
     (partial,) = call(inner_kernel, (block,), swept, [pad, z_part, in_vmem(partial)], "inner", {2: 0})
     partial = in_vmem(partial)
     work = [
@@ -339,9 +365,15 @@
         pltpu.SemaphoreType.DMA((FIELDS, 2, 2)),
     ]
     whole = pltpu.HBM((FIELDS, ROWS, LANES), f32)
-    half = call(half_kernel, whole, work, [partial, near_z, far_x, near_x], "half", None, any_spec())
+    half = call(half_kernel, whole, work, [pad, partial, far_z], "half", None, any_spec())
     return call(
-        edge_kernel, whole, work, [partial, far_z, near_z, far_x, near_x, half], "edges", {5: 0}, any_spec()
+        edge_kernel,
+        whole,
+        work,
+        [pad, partial, far_z, near_z, far_x, near_x, half],
+        "edges",
+        {6: 0},
+        any_spec(),
     )
 
 

time: 22.5 us -> 19.7 us (0.88); the launches traced: 22.1 us -> 19.7 us
  waiting for transfers between devices: 2.32 us -> 0.01 us
  Pallas kernels: 12.2 us -> 11.5 us
  starting transfers between devices: 7.6 us -> 8.06 us
    ppermute x4, waiting for transfers between devices: 2.32 us -> 0.01 us  [swap(): return lax.ppermute(value, axis, pairs + [(j, i) for i, j in pairs])]
    pallas_call x5 -> x6, Pallas kernels: 12.2 us -> 11.5 us  [call(): pl.pallas_call(kernel, out_shape=outs, in_specs=[any_spec() if value.ndim...]
    ppermute x4, starting transfers between devices: 7.6 us -> 8.06 us  [swap(): return lax.ppermute(value, axis, pairs + [(j, i) for i, j in pairs])]
  transfers between devices with their start and end apart: 4 -> 4, of which waited for: 1 -> 0; matrix products, arithmetic and copies ran while one was open for 0% -> 0% of each run, Pallas kernels for 32% -> 8%
where the time goes in v7:
time: 19.7 us
  Pallas kernels  11.5 us (58%)
  starting transfers between devices  8.06 us (41%)
    pallas_call x6, Pallas kernels, call(): pl.pallas_call(kernel, out_shape=outs, in_specs=[any_spec() if value.ndim...  11.5 us
    ppermute x4, starting transfers between devices, swap(): return lax.ppermute(value, axis, pairs + [(j, i) for i, j in pairs])  8.06 us
  transfers between devices with their start and end apart: 4, of which 0 were waited for; matrix products, arithmetic and copies ran while one was open for 0% of the time, Pallas kernels for 8%

profile of v7, /device:TPU:1, one launch (start us, length us, event | category | flops | bytes accessed | tf_op | source)
XLA Modules:
  0.0 19.7 jit_solution(10422082455074385777)
XLA Ops:
  0.0 3.1 %pack.1 = (f32[4,2,1576,128]{3,2,1,0:T(8,128)S(1)}, f32[1,2,1544,128]{3,2,1,0:T(8,128)S(1)}, f32[8,256]{1,0:T(8,128)S(1)}, f32[8,256]{1,0:T(8,128)S(1)}, f32[152,128]{1,0:T(8,128)S(1)}, /*index=5*/f32[160,128]{1,0:T(8,128)S(1)}) custom-call(f32[4,1536,256]{2,1,0:T(8,128)} %v_hbm.1), custom_call_target="tpu_custom_call" | custom-call | tf_op jit(solution)/shard_map/pack/pallas_call | solution.py:307
  3.2 3.8 %first.1 = (f32[4,2,1544,128]{3,2,1,0:T(8,128)S(1)}, f32[160,128]{1,0:T(8,128)S(1)}) custom-call(f32[4,2,1576,128]{3,2,1,0:T(8,128)S(1)} %get-tuple-element.17.pad, f32[1,2,1544,128]{3,2,1,0:T(8,128)S(1)} %get-tuple-element.18.z_part, f32[160,128]{1,0:T(8,128)S(1)} %get-tuple-element.19.far_z_in), custom_call_target="tpu_custom_call", output_to_operand_aliasing={{1}: (2, {})} | custom-call | tf_op jit(solution)/shard_map/first/pallas_call | solution.py:307
  6.9 4.9 %collective-permute-start = (f32[160,128]{1,0:T(8,128)S(1)}, f32[160,128]{1,0:T(8,128)S(1)}, u32[]{:S(2)}, u32[]{:S(2)}) collective-permute-start(f32[160,128]{1,0:T(8,128)S(1)} %get-tuple-element.25), channel_id=1, source_target_pairs={{1,2},{3,4},{5,6},{7,8},{9,10},{11,12},{13,14},{15,16},{17,18},{19... | collective-permute-start | bytes 245768 | tf_op jit(solution)/shard_map/ppermute | solution.py:344
  11.9 0.0 collective-permute-start.1
  11.9 2.2 %collective-permute-start.2 = (f32[8,256]{1,0:T(8,128)S(1)}, f32[8,256]{1,0:T(8,128)S(1)}, u32[]{:S(2)}, u32[]{:S(2)}) collective-permute-start(f32[8,256]{1,0:T(8,128)S(1)} %get-tuple-element.27), channel_id=1, source_target_pairs={{32,64},{96,128},{160,192},{224,0},{64,32},{128,96},{192,160},{0,2... | collective-permute-start | bytes 24584 | tf_op jit(solution)/shard_map/ppermute | solution.py:344
  14.0 1.0 %collective-permute-start.3 = (f32[8,256]{1,0:T(8,128)S(1)}, f32[8,256]{1,0:T(8,128)S(1)}, u32[]{:S(2)}, u32[]{:S(2)}) collective-permute-start(f32[8,256]{1,0:T(8,128)S(1)} %get-tuple-element.28), channel_id=1, source_target_pairs={{0,32},{64,96},{128,160},{192,224},{32,0},{96,64},{160,128},{224,1... | collective-permute-start | bytes 24584 | tf_op jit(solution)/shard_map/ppermute | solution.py:344
  15.0 1.4 %inner.1 = f32[4,2,1544,128]{3,2,1,0:T(8,128)S(1)} custom-call(f32[4,2,1576,128]{3,2,1,0:T(8,128)S(1)} %get-tuple-element.17.pad, f32[1,2,1544,128]{3,2,1,0:T(8,128)S(1)} %get-tuple-element.18.z_part, f32[4,2,1544,128]{3,2,1,0:T(8,128)S(1)} %get-tuple-element.24.done), custom_call_target="tpu_custom_call", output_to_operand_aliasing={{}: (2, {})} | custom-call | tf_op jit(solution)/shard_map/inner/pallas_call | solution.py:307
  16.5 0.0 collective-permute-done.far_z
  16.5 0.2 half.1
  16.6 0.0 collective-permute-done.2.far_x
  16.6 0.0 collective-permute-done.3.near_x
  16.6 0.0 collective-permute-done.1.near_z
  16.7 3.0 %edges.1 = f32[4,1536,256]{2,1,0:T(8,128)} custom-call(f32[4,2,1576,128]{3,2,1,0:T(8,128)S(1)} %get-tuple-element.17.pad, f32[4,2,1544,128]{3,2,1,0:T(8,128)S(1)} %inner.1, f32[160,128]{1,0:T(8,128)S(1)} %collective-permute-done.far_z, f32[152,128]{1,0:T(8,128)S(1)} %collective-permute-done.1.near_z, ...), custom_call_target="tpu_custom_call", output_to_operand_aliasing={{}: (6, {})} | custom-call | tf_op jit(solution)/shard_map/edges/pallas_call | solution.py:307
  (1 shorter events, 0.0 us)
Async XLA Ops:
  6.9 9.5 %collective-permute-start = (f32[160,128]{1,0:T(8,128)S(1)}, f32[160,128]{1,0:T(8,128)S(1)}, u32[]{:S(2)}, u32[]{:S(2)}) collective-permute-start(f32[160,128]{1,0:T(8,128)S(1)} %get-tuple-element.25), channel_id=1, source_target_pairs={{1,2},{3,4},{5,6},{7,8},{9,10},{11,12},{13,14},{15,16},{17,18},{19... | collective-permute-start | bytes 245768 | tf_op jit(solution)/shard_map/ppermute | solution.py:344
  11.9 4.8 %collective-permute-start.1 = (f32[152,128]{1,0:T(8,128)S(1)}, f32[152,128]{1,0:T(8,128)S(1)}, u32[]{:S(2)}, u32[]{:S(2)}) collective-permute-start(f32[152,128]{1,0:T(8,128)S(1)} %get-tuple-element.26), channel_id=1, source_target_pairs={{0,1},{2,3},{4,5},{6,7},{8,9},{10,11},{12,13},{14,15},{16,17},{18,... | collective-permute-start | bytes 233480 | tf_op jit(solution)/shard_map/ppermute | solution.py:344
  11.9 4.8 %collective-permute-start.2 = (f32[8,256]{1,0:T(8,128)S(1)}, f32[8,256]{1,0:T(8,128)S(1)}, u32[]{:S(2)}, u32[]{:S(2)}) collective-permute-start(f32[8,256]{1,0:T(8,128)S(1)} %get-tuple-element.27), channel_id=1, source_target_pairs={{32,64},{96,128},{160,192},{224,0},{64,32},{128,96},{192,160},{0,2... | collective-permute-start | bytes 24584 | tf_op jit(solution)/shard_map/ppermute | solution.py:344
  14.0 2.6 %collective-permute-start.3 = (f32[8,256]{1,0:T(8,128)S(1)}, f32[8,256]{1,0:T(8,128)S(1)}, u32[]{:S(2)}, u32[]{:S(2)}) collective-permute-start(f32[8,256]{1,0:T(8,128)S(1)} %get-tuple-element.28), channel_id=1, source_target_pairs={{0,32},{64,96},{128,160},{192,224},{32,0},{96,64},{160,128},{224,1... | collective-permute-start | bytes 24584 | tf_op jit(solution)/shard_map/ppermute | solution.py:344

commit v8 on v7

--- a/solution.py
+++ b/solution.py
@@ -279,7 +279,7 @@
         finish((), (), (1,), False, pad, inner, None, None, out_hbm, work, turned_out, sems)
 
 
-def edge_kernel(pad, inner, far_z, near_z, far_x, near_x, half, out_hbm, work, turned_in, turned_out, sems):
+def edge_kernel(pad, inner, near_x, far_x, far_z, near_z, half, out_hbm, work, turned_in, turned_out, sems):
     even_x, even_z = is_even("gx"), is_even("gz")
     before = jnp.where(even_x, far_x[...], near_x[...])
     after = jnp.where(even_x, near_x[...], far_x[...])
@@ -370,7 +370,7 @@
         edge_kernel,
         whole,
         work,
-        [pad, partial, far_z, near_z, far_x, near_x, half],
+        [pad, partial, near_x, far_x, far_z, near_z, half],
         "edges",
         {6: 0},
         any_spec(),

time: 19.7 us -> 19.4 us (0.985)
  starting transfers between devices: 8.06 us -> 7.09 us
  waiting for transfers between devices: 0.01 us -> 0.56 us
    ppermute x4, starting transfers between devices: 8.06 us -> 7.09 us  [swap(): return lax.ppermute(value, axis, pairs + [(j, i) for i, j in pairs])]
    ppermute x4, waiting for transfers between devices: 0.01 us -> 0.56 us  [swap(): return lax.ppermute(value, axis, pairs + [(j, i) for i, j in pairs])]
  transfers between devices with their start and end apart: 4 -> 4, of which waited for: 0 -> 1; matrix products, arithmetic and copies ran while one was open for 0% -> 0% of each run, Pallas kernels for 8% -> 8%
where the time goes in v8:
time: 19.4 us; the launch traced here: 19.2 us
  Pallas kernels  11.5 us (59%)
  starting transfers between devices  7.09 us (37%)
  waiting for transfers between devices  0.56 us (3%)
    pallas_call x6, Pallas kernels, call(): pl.pallas_call(kernel, out_shape=outs, in_specs=[any_spec() if value.ndim...  11.5 us
    ppermute x4, starting transfers between devices, swap(): return lax.ppermute(value, axis, pairs + [(j, i) for i, j in pairs])  7.09 us
    ppermute x4, waiting for transfers between devices, swap(): return lax.ppermute(value, axis, pairs + [(j, i) for i, j in pairs])  0.56 us
  transfers between devices with their start and end apart: 4, of which 1 were waited for; matrix products, arithmetic and copies ran while one was open for 0% of the time, Pallas kernels for 8%

profile of v8, /device:TPU:1, one launch (start us, length us, event | category | flops | bytes accessed | tf_op | source)
XLA Modules:
  0.0 19.2 jit_solution(18163127407427104943)
XLA Ops:
  0.0 3.1 %pack.1 = (f32[4,2,1576,128]{3,2,1,0:T(8,128)S(1)}, f32[1,2,1544,128]{3,2,1,0:T(8,128)S(1)}, f32[8,256]{1,0:T(8,128)S(1)}, f32[8,256]{1,0:T(8,128)S(1)}, f32[152,128]{1,0:T(8,128)S(1)}, /*index=5*/f32[160,128]{1,0:T(8,128)S(1)}) custom-call(f32[4,1536,256]{2,1,0:T(8,128)} %v_hbm.1), custom_call_target="tpu_custom_call" | custom-call | tf_op jit(solution)/shard_map/pack/pallas_call | solution.py:307
  3.2 3.8 %first.1 = (f32[4,2,1544,128]{3,2,1,0:T(8,128)S(1)}, f32[160,128]{1,0:T(8,128)S(1)}) custom-call(f32[4,2,1576,128]{3,2,1,0:T(8,128)S(1)} %get-tuple-element.17.pad, f32[1,2,1544,128]{3,2,1,0:T(8,128)S(1)} %get-tuple-element.18.z_part, f32[160,128]{1,0:T(8,128)S(1)} %get-tuple-element.19.far_z_in), custom_call_target="tpu_custom_call", output_to_operand_aliasing={{1}: (2, {})} | custom-call | tf_op jit(solution)/shard_map/first/pallas_call | solution.py:307
  6.9 4.9 %collective-permute-start.2 = (f32[160,128]{1,0:T(8,128)S(1)}, f32[160,128]{1,0:T(8,128)S(1)}, u32[]{:S(2)}, u32[]{:S(2)}) collective-permute-start(f32[160,128]{1,0:T(8,128)S(1)} %get-tuple-element.27), channel_id=1, source_target_pairs={{1,2},{3,4},{5,6},{7,8},{9,10},{11,12},{13,14},{15,16},{17,18},{19... | collective-permute-start | bytes 245768 | tf_op jit(solution)/shard_map/ppermute | solution.py:344
  11.9 0.0 collective-permute-start.3
  11.9 1.0 %collective-permute-start = (f32[8,256]{1,0:T(8,128)S(1)}, f32[8,256]{1,0:T(8,128)S(1)}, u32[]{:S(2)}, u32[]{:S(2)}) collective-permute-start(f32[8,256]{1,0:T(8,128)S(1)} %get-tuple-element.25), channel_id=1, source_target_pairs={{0,32},{64,96},{128,160},{192,224},{32,0},{96,64},{160,128},{224,1... | collective-permute-start | bytes 24584 | tf_op jit(solution)/shard_map/ppermute | solution.py:344
  12.9 1.2 %collective-permute-start.1 = (f32[8,256]{1,0:T(8,128)S(1)}, f32[8,256]{1,0:T(8,128)S(1)}, u32[]{:S(2)}, u32[]{:S(2)}) collective-permute-start(f32[8,256]{1,0:T(8,128)S(1)} %get-tuple-element.26), channel_id=1, source_target_pairs={{32,64},{96,128},{160,192},{224,0},{64,32},{128,96},{192,160},{0,2... | collective-permute-start | bytes 24584 | tf_op jit(solution)/shard_map/ppermute | solution.py:344
  14.0 1.4 %inner.1 = f32[4,2,1544,128]{3,2,1,0:T(8,128)S(1)} custom-call(f32[4,2,1576,128]{3,2,1,0:T(8,128)S(1)} %get-tuple-element.17.pad, f32[1,2,1544,128]{3,2,1,0:T(8,128)S(1)} %get-tuple-element.18.z_part, f32[4,2,1544,128]{3,2,1,0:T(8,128)S(1)} %get-tuple-element.24.done), custom_call_target="tpu_custom_call", output_to_operand_aliasing={{}: (2, {})} | custom-call | tf_op jit(solution)/shard_map/inner/pallas_call | solution.py:307
  15.5 0.0 collective-permute-done.2.far_z
  15.5 0.2 half.1
  15.7 0.0 collective-permute-done.near_x
  15.7 0.5 %collective-permute-done.1.far_x = f32[8,256]{1,0:T(8,128)S(1)} collective-permute-done((f32[8,256]{1,0:T(8,128)S(1)}, f32[8,256]{1,0:T(8,128)S(1)}, u32[]{:S(2)}, u32[]{:S(2)}) %collective-permute-start.1) | collective-permute-done | bytes 8224 | tf_op jit(solution)/shard_map/ppermute | solution.py:344
  16.2 0.0 collective-permute-done.3.near_z
  16.2 3.0 %edges.1 = f32[4,1536,256]{2,1,0:T(8,128)} custom-call(f32[4,2,1576,128]{3,2,1,0:T(8,128)S(1)} %get-tuple-element.17.pad, f32[4,2,1544,128]{3,2,1,0:T(8,128)S(1)} %inner.1, f32[8,256]{1,0:T(8,128)S(1)} %collective-permute-done.near_x, f32[8,256]{1,0:T(8,128)S(1)} %collective-permute-done.1.far_x, ...), custom_call_target="tpu_custom_call", output_to_operand_aliasing={{}: (6, {})} | custom-call | tf_op jit(solution)/shard_map/edges/pallas_call | solution.py:307
  (1 shorter events, 0.0 us)
Async XLA Ops:
  6.9 8.6 %collective-permute-start.2 = (f32[160,128]{1,0:T(8,128)S(1)}, f32[160,128]{1,0:T(8,128)S(1)}, u32[]{:S(2)}, u32[]{:S(2)}) collective-permute-start(f32[160,128]{1,0:T(8,128)S(1)} %get-tuple-element.27), channel_id=1, source_target_pairs={{1,2},{3,4},{5,6},{7,8},{9,10},{11,12},{13,14},{15,16},{17,18},{19... | collective-permute-start | bytes 245768 | tf_op jit(solution)/shard_map/ppermute | solution.py:344
  11.9 4.4 %collective-permute-start.3 = (f32[152,128]{1,0:T(8,128)S(1)}, f32[152,128]{1,0:T(8,128)S(1)}, u32[]{:S(2)}, u32[]{:S(2)}) collective-permute-start(f32[152,128]{1,0:T(8,128)S(1)} %get-tuple-element.28), channel_id=1, source_target_pairs={{0,1},{2,3},{4,5},{6,7},{8,9},{10,11},{12,13},{14,15},{16,17},{18,... | collective-permute-start | bytes 233480 | tf_op jit(solution)/shard_map/ppermute | solution.py:344
  11.9 3.8 %collective-permute-start = (f32[8,256]{1,0:T(8,128)S(1)}, f32[8,256]{1,0:T(8,128)S(1)}, u32[]{:S(2)}, u32[]{:S(2)}) collective-permute-start(f32[8,256]{1,0:T(8,128)S(1)} %get-tuple-element.25), channel_id=1, source_target_pairs={{0,32},{64,96},{128,160},{192,224},{32,0},{96,64},{160,128},{224,1... | collective-permute-start | bytes 24584 | tf_op jit(solution)/shard_map/ppermute | solution.py:344
  12.9 3.4 %collective-permute-start.1 = (f32[8,256]{1,0:T(8,128)S(1)}, f32[8,256]{1,0:T(8,128)S(1)}, u32[]{:S(2)}, u32[]{:S(2)}) collective-permute-start(f32[8,256]{1,0:T(8,128)S(1)} %get-tuple-element.26), channel_id=1, source_target_pairs={{32,64},{96,128},{160,192},{224,0},{64,32},{128,96},{192,160},{0,2... | collective-permute-start | bytes 24584 | tf_op jit(solution)/shard_map/ppermute | solution.py:344

commit v9 on v8

--- a/solution.py
+++ b/solution.py
@@ -73,51 +73,97 @@
     return lax.rem(lax.axis_index(axis), 2) == 0
 
 
+def fetch(v_hbm, pad, sides, sems):
+    copies = {}
+    for f in range(FIELDS):
+        for c in sides:
+            lanes = pl.ds(c * TILE, TILE)
+            copies[f, c] = pltpu.make_async_copy(v_hbm.at[f, :, lanes], pad.at[f, c, pl.ds(HALO, ROWS)], sems.at[f, c])
+            copies[f, c].start()
+
+    def wait(f):
+        for c in sides:
+            copies[f, c].wait()
+
+    return wait
+
+
+def pack_x(f, pad, near_x, far_x):
+    even_x = is_even("gx")
+    place = lax.broadcasted_iota(jnp.int32, (HALO, TILE), 0)
+    head_weight, tail_weight = powers(place + 1), powers(HALO - place)
+    for c in range(2):
+        lanes = pl.ds(c * TILE, TILE)
+        head, tail = pad[f, c, pl.ds(HALO, HALO)], pad[f, c, pl.ds(ROWS, HALO)]
+        head_sum = jnp.sum(head * head_weight, axis=0, keepdims=True)
+        tail_sum = jnp.sum(tail * tail_weight, axis=0, keepdims=True)
+        near_x[pl.ds(2 * f, 1), lanes] = jnp.where(even_x, tail_sum, head_sum)
+        far_x[pl.ds(2 * f, 1), lanes] = jnp.where(even_x, head_sum, tail_sum)
+        near_x[pl.ds(2 * f + 1, 1), lanes] = jnp.where(even_x, tail[HALO - 1 :], head[:1])
+        far_x[pl.ds(2 * f + 1, 1), lanes] = jnp.where(even_x, head[:1], tail[HALO - 1 :])
+
+
+def turn(f, pad, sides, turned_first, turned_last):
+    lane = lax.broadcasted_iota(jnp.int32, (TILE, TILE), 1)
+    for b in range(BLOCKS):
+        rows = pl.ds(HALO + b * TILE, TILE)
+        tile = pad[f, sides[0], rows]
+        if len(sides) == 2:
+            tile = jnp.where(lane < 64, tile, pad[f, 1, rows])
+        turned = tile.T
+        block = f * BLOCKS + b
+        if 0 in sides:
+            turned_first[pl.ds(block, SUB, stride=GAP)] = turned[:SUB]
+        if 1 in sides:
+            turned_last[pl.ds(block + 3, SUB, stride=GAP)] = turned[TILE - SUB :]
+
+
+def early_spanwise(f, pad, z_part):
+    if f >= EARLY:
+        return
+    matrix = difference_matrix()
+    for b in range(0, ROWS, 256):
+        total = spanwise(field_rows(pad, f, b, 256), matrix)
+        z_part[f, 0, pl.ds(b, 256)] = total[:, :TILE]
+        z_part[f, 1, pl.ds(b, 256)] = total[:, TILE:]
+
+
+def last_columns(turned_last):
+    return turned_last[5 * GAP + 3 : 5 * GAP + 3 + EDGE]
+
+
+def is_awaited():
+    return place_z() == lax.axis_size("gz") - 1
+
+
 def pack_kernel(v_hbm, pad, z_part, near_x, far_x, near_z, far_z, turned_first, turned_last, sems):
-    copies = []
-    for f in range(FIELDS):
-        for c in range(2):
-            lanes = pl.ds(c * TILE, TILE)
-            copy = pltpu.make_async_copy(v_hbm.at[f, :, lanes], pad.at[f, c, pl.ds(HALO, ROWS)], sems.at[f, c])
-            copy.start()
-            copies.append(copy)
-    even_x, even_z = is_even("gx"), is_even("gz")
-    matrix = difference_matrix()
     zeros = jnp.zeros((HALO, TILE), jnp.float32)
     for f in range(FIELDS):
         for c in range(2):
             pad[f, c, pl.ds(0, HALO)] = zeros
             pad[f, c, pl.ds(HALO + ROWS, PAD - HALO - ROWS)] = jnp.zeros((PAD - HALO - ROWS, TILE), jnp.float32)
-    lane = lax.broadcasted_iota(jnp.int32, (TILE, TILE), 1)
-    place = lax.broadcasted_iota(jnp.int32, (HALO, TILE), 0)
-    head_weight, tail_weight = powers(place + 1), powers(HALO - place)
-    for f in range(FIELDS):
-        for c in range(2):
-            copies[2 * f + c].wait()
-        for c in range(2):
-            lanes = pl.ds(c * TILE, TILE)
-            head, tail = pad[f, c, pl.ds(HALO, HALO)], pad[f, c, pl.ds(ROWS, HALO)]
-            head_sum = jnp.sum(head * head_weight, axis=0, keepdims=True)
-            tail_sum = jnp.sum(tail * tail_weight, axis=0, keepdims=True)
-            near_x[pl.ds(2 * f, 1), lanes] = jnp.where(even_x, tail_sum, head_sum)
-            far_x[pl.ds(2 * f, 1), lanes] = jnp.where(even_x, head_sum, tail_sum)
-            near_x[pl.ds(2 * f + 1, 1), lanes] = jnp.where(even_x, tail[HALO - 1 :], head[:1])
-            far_x[pl.ds(2 * f + 1, 1), lanes] = jnp.where(even_x, head[:1], tail[HALO - 1 :])
-        for b in range(BLOCKS):
-            rows = pl.ds(HALO + b * TILE, TILE)
-            turned = jnp.where(lane < 64, pad[f, 0, rows], pad[f, 1, rows]).T
-            block = f * BLOCKS + b
-            turned_first[pl.ds(block, SUB, stride=GAP)] = turned[:SUB]
-            turned_last[pl.ds(block + 3, SUB, stride=GAP)] = turned[TILE - SUB :]
-        if f < EARLY:
-            for b in range(0, ROWS, 256):
-                total = spanwise(field_rows(pad, f, b, 256), matrix)
-                z_part[f, 0, pl.ds(b, 256)] = total[:, :TILE]
-                z_part[f, 1, pl.ds(b, 256)] = total[:, TILE:]
-    first, last = turned_first[0:EDGE], turned_last[5 * GAP + 3 : 5 * GAP + 3 + EDGE]
-    near_z[...] = jnp.where(even_z, last, first)
-    far_z[0:EDGE] = jnp.where(even_z, first, last)
     far_z[EDGE:] = jnp.zeros((FAR_EDGE - EDGE, TILE), jnp.float32)
+
+    @pl.when(is_awaited())
+    def _():
+        wait = fetch(v_hbm, pad, (1,), sems)
+        for f in range(FIELDS):
+            wait(f)
+            turn(f, pad, (1,), turned_first, turned_last)
+        far_z[0:EDGE] = last_columns(turned_last)
+
+    @pl.when(jnp.logical_not(is_awaited()))
+    def _():
+        wait = fetch(v_hbm, pad, (0, 1), sems)
+        for f in range(FIELDS):
+            wait(f)
+            pack_x(f, pad, near_x, far_x)
+            turn(f, pad, (0, 1), turned_first, turned_last)
+            early_spanwise(f, pad, z_part)
+        even_z = is_even("gz")
+        first, last = turned_first[0:EDGE], last_columns(turned_last)
+        near_z[...] = jnp.where(even_z, last, first)
+        far_z[0:EDGE] = jnp.where(even_z, first, last)
 
 
 def inner_body(pad, z_part, out, swept):
@@ -190,11 +236,24 @@
     pl.when(place_z() == 0)(lambda: inner_body(pad, z_part, out, swept))
 
 
-def second_kernel(pad, z_part, done, near_z_in, near_x_in, far_x_in, out, near_z, near_x, far_x, swept):
+def second_kernel(
+    pad_in, z_part_in, done, near_z_in, near_x_in, far_x_in, v_hbm,
+    out, near_z, near_x, far_x, pad, z_part, swept, turned_first, turned_last, sems,
+):
     @pl.when(place_z() == 1)
     def _():
         inner_body(pad, z_part, out, swept)
         add_spanwise(pad, out, range(MIDDLE, FIELDS))
+
+    @pl.when(is_awaited())
+    def _():
+        wait = fetch(v_hbm, pad, (0,), sems)
+        for f in range(FIELDS):
+            wait(f)
+            pack_x(f, pad, near_x, far_x)
+            turn(f, pad, (0,), turned_first, turned_last)
+            early_spanwise(f, pad, z_part)
+        near_z[...] = turned_first[0:EDGE]
 
 
 def inner_kernel(pad, z_part, done, out, swept):
@@ -323,19 +382,12 @@
     far_edge = pltpu.VMEM((FAR_EDGE, TILE), f32)
     turned = pltpu.VMEM((400, TILE), f32)
     swept = [pltpu.VMEM((2 * FIELDS, STEPS * SUB, TILE), f32)]
+    packing = [turned, turned, pltpu.SemaphoreType.DMA((FIELDS, 2))]
+    pad_type = pltpu.VMEM((FIELDS, 2, PAD, TILE), f32)
+    z_part_type = pltpu.VMEM((EARLY, 2, LONG, TILE), f32)
+    source = pltpu.with_memory_space_constraint(velocity, pltpu.HBM)
     pad, z_part, near_x, far_x, near_z, far_z = call(
-        pack_kernel,
-        (
-            pltpu.VMEM((FIELDS, 2, PAD, TILE), f32),
-            pltpu.VMEM((EARLY, 2, LONG, TILE), f32),
-            x_edge,
-            x_edge,
-            z_edge,
-            far_edge,
-        ),
-        [turned, turned, pltpu.SemaphoreType.DMA((FIELDS, 2))],
-        [pltpu.with_memory_space_constraint(velocity, pltpu.HBM)],
-        "pack",
+        pack_kernel, (pad_type, z_part_type, x_edge, x_edge, z_edge, far_edge), packing, [source], "pack"
     )
 
     def swap(value, axis, first):
@@ -346,14 +398,15 @@
     pad, z_part = in_vmem(pad), in_vmem(z_part)
     partial, far_z = call(first_kernel, (block, far_edge), swept, [pad, z_part, in_vmem(far_z)], "first", {2: 1})
     far_z = swap(far_z, "gz", 1)
-    partial, near_z, near_x, far_x = call(
+    partial, near_z, near_x, far_x, pad, z_part = call(
         second_kernel,
-        (block, z_edge, x_edge, x_edge),
-        swept,
-        [pad, z_part, in_vmem(partial), in_vmem(near_z), in_vmem(near_x), in_vmem(far_x)],
+        (block, z_edge, x_edge, x_edge, pad_type, z_part_type),
+        swept + packing,
+        [pad, z_part, in_vmem(partial), in_vmem(near_z), in_vmem(near_x), in_vmem(far_x), source],
         "second",
-        {2: 0, 3: 1, 4: 2, 5: 3},
+        {2: 0, 3: 1, 4: 2, 5: 3, 0: 4, 1: 5},
     )
+    pad, z_part = in_vmem(pad), in_vmem(z_part)
     near_z = swap(near_z, "gz", 0)
     near_x, far_x = swap(near_x, "gx", 0), swap(far_x, "gx", 1)
     (partial,) = call(inner_kernel, (block,), swept, [pad, z_part, in_vmem(partial)], "inner", {2: 0})

time: 19.4 us -> 19.8 us (1.021)
  Pallas kernels: 11.5 us -> 11.8 us
    pallas_call x6, Pallas kernels: 11.5 us -> 11.8 us  [call(): pl.pallas_call(kernel, out_shape=outs, in_specs=[any_spec() if value.ndim...]
where the time goes in v9:
time: 19.8 us; the launch traced here: 19.7 us
  Pallas kernels  11.8 us (60%)
  starting transfers between devices  7.08 us (36%)
  waiting for transfers between devices  0.56 us (3%)
  between operations  0.22 us (1%)
    pallas_call x6, Pallas kernels, call(): pl.pallas_call(kernel, out_shape=outs, in_specs=[any_spec() if value.ndim...  11.8 us
    ppermute x4, starting transfers between devices, swap(): return lax.ppermute(value, axis, pairs + [(j, i) for i, j in pairs])  7.08 us
    ppermute x4, waiting for transfers between devices, swap(): return lax.ppermute(value, axis, pairs + [(j, i) for i, j in pairs])  0.56 us
  transfers between devices with their start and end apart: 4, of which 1 were waited for; matrix products, arithmetic and copies ran while one was open for 0% of the time, Pallas kernels for 8%

profile of v9, /device:TPU:1, one launch (start us, length us, event | category | flops | bytes accessed | tf_op | source)
XLA Modules:
  0.0 19.7 jit_solution(7112201278974252163)
XLA Ops:
  0.0 3.2 %pack.1 = (f32[4,2,1576,128]{3,2,1,0:T(8,128)S(1)}, f32[1,2,1544,128]{3,2,1,0:T(8,128)S(1)}, f32[8,256]{1,0:T(8,128)S(1)}, f32[8,256]{1,0:T(8,128)S(1)}, f32[152,128]{1,0:T(8,128)S(1)}, /*index=5*/f32[160,128]{1,0:T(8,128)S(1)}) custom-call(f32[4,1536,256]{2,1,0:T(8,128)} %v_hbm.3), custom_call_target="tpu_custom_call" | custom-call | tf_op jit(solution)/shard_map/pack/pallas_call | solution.py:366
  3.2 3.8 %first.1 = (f32[4,2,1544,128]{3,2,1,0:T(8,128)S(1)}, f32[160,128]{1,0:T(8,128)S(1)}) custom-call(f32[4,2,1576,128]{3,2,1,0:T(8,128)S(1)} %get-tuple-element.19.pad.pad_in, f32[1,2,1544,128]{3,2,1,0:T(8,128)S(1)} %get-tuple-element.20.z_part.z_part_in, f32[160,128]{1,0:T(8,128)S(1)} %get-tuple-element.21.far_z_in), custom_call_target="tpu_custom_call", output_to_operand_aliasing={{1}: (2, {})} | custom-call | tf_op jit(solution)/shard_map/first/pallas_call | solution.py:366
  7.0 4.0 %collective-permute-start.2 = (f32[160,128]{1,0:T(8,128)S(1)}, f32[160,128]{1,0:T(8,128)S(1)}, u32[]{:S(2)}, u32[]{:S(2)}) collective-permute-start(f32[160,128]{1,0:T(8,128)S(1)} %get-tuple-element.31), channel_id=1, source_target_pairs={{1,2},{3,4},{5,6},{7,8},{9,10},{11,12},{13,14},{15,16},{17,18},{19... | collective-permute-start | bytes 245768 | tf_op jit(solution)/shard_map/ppermute | solution.py:396
  11.0 0.1 second.1
  11.1 0.6 %collective-permute-start.3 = (f32[152,128]{1,0:T(8,128)S(1)}, f32[152,128]{1,0:T(8,128)S(1)}, u32[]{:S(2)}, u32[]{:S(2)}) collective-permute-start(f32[152,128]{1,0:T(8,128)S(1)} %get-tuple-element.32), channel_id=1, source_target_pairs={{0,1},{2,3},{4,5},{6,7},{8,9},{10,11},{12,13},{14,15},{16,17},{18,... | collective-permute-start | bytes 233480 | tf_op jit(solution)/shard_map/ppermute | solution.py:396
  11.7 1.2 %collective-permute-start = (f32[8,256]{1,0:T(8,128)S(1)}, f32[8,256]{1,0:T(8,128)S(1)}, u32[]{:S(2)}, u32[]{:S(2)}) collective-permute-start(f32[8,256]{1,0:T(8,128)S(1)} %get-tuple-element.29), channel_id=1, source_target_pairs={{0,32},{64,96},{128,160},{192,224},{32,0},{96,64},{160,128},{224,1... | collective-permute-start | bytes 24584 | tf_op jit(solution)/shard_map/ppermute | solution.py:396
  13.0 1.2 %collective-permute-start.1 = (f32[8,256]{1,0:T(8,128)S(1)}, f32[8,256]{1,0:T(8,128)S(1)}, u32[]{:S(2)}, u32[]{:S(2)}) collective-permute-start(f32[8,256]{1,0:T(8,128)S(1)} %get-tuple-element.30), channel_id=1, source_target_pairs={{32,64},{96,128},{160,192},{224,0},{64,32},{128,96},{192,160},{0,2... | collective-permute-start | bytes 24584 | tf_op jit(solution)/shard_map/ppermute | solution.py:396
  14.2 1.4 %inner.1 = f32[4,2,1544,128]{3,2,1,0:T(8,128)S(1)} custom-call(f32[4,2,1576,128]{3,2,1,0:T(8,128)S(1)} %get-tuple-element.26.pad, f32[1,2,1544,128]{3,2,1,0:T(8,128)S(1)} %get-tuple-element.27.z_part, f32[4,2,1544,128]{3,2,1,0:T(8,128)S(1)} %get-tuple-element.28.done), custom_call_target="tpu_custom_call", output_to_operand_aliasing={{}: (2, {})} | custom-call | tf_op jit(solution)/shard_map/inner/pallas_call | solution.py:366
  15.6 0.0 collective-permute-done.2.far_z
  15.6 0.2 half.1
  15.8 0.0 collective-permute-done.near_x
  15.8 0.6 %collective-permute-done.1.far_x = f32[8,256]{1,0:T(8,128)S(1)} collective-permute-done((f32[8,256]{1,0:T(8,128)S(1)}, f32[8,256]{1,0:T(8,128)S(1)}, u32[]{:S(2)}, u32[]{:S(2)}) %collective-permute-start.1) | collective-permute-done | bytes 8224 | tf_op jit(solution)/shard_map/ppermute | solution.py:396
  16.3 0.0 collective-permute-done.3.near_z
  16.4 3.2 %edges.1 = f32[4,1536,256]{2,1,0:T(8,128)} custom-call(f32[4,2,1576,128]{3,2,1,0:T(8,128)S(1)} %get-tuple-element.26.pad, f32[4,2,1544,128]{3,2,1,0:T(8,128)S(1)} %inner.1, f32[8,256]{1,0:T(8,128)S(1)} %collective-permute-done.near_x, f32[8,256]{1,0:T(8,128)S(1)} %collective-permute-done.1.far_x, ...), custom_call_target="tpu_custom_call", output_to_operand_aliasing={{}: (6, {})} | custom-call | tf_op jit(solution)/shard_map/edges/pallas_call | solution.py:366
Async XLA Ops:
  7.0 8.6 %collective-permute-start.2 = (f32[160,128]{1,0:T(8,128)S(1)}, f32[160,128]{1,0:T(8,128)S(1)}, u32[]{:S(2)}, u32[]{:S(2)}) collective-permute-start(f32[160,128]{1,0:T(8,128)S(1)} %get-tuple-element.31), channel_id=1, source_target_pairs={{1,2},{3,4},{5,6},{7,8},{9,10},{11,12},{13,14},{15,16},{17,18},{19... | collective-permute-start | bytes 245768 | tf_op jit(solution)/shard_map/ppermute | solution.py:396
  11.1 5.2 %collective-permute-start.3 = (f32[152,128]{1,0:T(8,128)S(1)}, f32[152,128]{1,0:T(8,128)S(1)}, u32[]{:S(2)}, u32[]{:S(2)}) collective-permute-start(f32[152,128]{1,0:T(8,128)S(1)} %get-tuple-element.32), channel_id=1, source_target_pairs={{0,1},{2,3},{4,5},{6,7},{8,9},{10,11},{12,13},{14,15},{16,17},{18,... | collective-permute-start | bytes 233480 | tf_op jit(solution)/shard_map/ppermute | solution.py:396
  11.7 4.0 %collective-permute-start = (f32[8,256]{1,0:T(8,128)S(1)}, f32[8,256]{1,0:T(8,128)S(1)}, u32[]{:S(2)}, u32[]{:S(2)}) collective-permute-start(f32[8,256]{1,0:T(8,128)S(1)} %get-tuple-element.29), channel_id=1, source_target_pairs={{0,32},{64,96},{128,160},{192,224},{32,0},{96,64},{160,128},{224,1... | collective-permute-start | bytes 24584 | tf_op jit(solution)/shard_map/ppermute | solution.py:396
  13.0 3.4 %collective-permute-start.1 = (f32[8,256]{1,0:T(8,128)S(1)}, f32[8,256]{1,0:T(8,128)S(1)}, u32[]{:S(2)}, u32[]{:S(2)}) collective-permute-start(f32[8,256]{1,0:T(8,128)S(1)} %get-tuple-element.30), channel_id=1, source_target_pairs={{32,64},{96,128},{160,192},{224,0},{64,32},{128,96},{192,160},{0,2... | collective-permute-start | bytes 24584 | tf_op jit(solution)/shard_map/ppermute | solution.py:396

commit v10 on v7

--- a/solution.py
+++ b/solution.py
@@ -199,7 +199,6 @@
 
 def inner_kernel(pad, z_part, done, out, swept):
     pl.when(place_z() > 1)(lambda: inner_body(pad, z_part, out, swept))
-    pl.when(place_z() == 0)(lambda: add_spanwise(pad, out, range(MIDDLE, FIELDS)))
 
 
 def halo_columns(left, right, turned_in, turned_out):
@@ -286,9 +285,8 @@
     near, far = near_z[...], far_z[0:EDGE]
     halo_columns(jnp.where(even_z, far, near), jnp.where(even_z, near, far), turned_in, turned_out)
     rest = (pad, inner, before, after, out_hbm, work, turned_out, sems)
-    pl.when(place_z() == 0)(lambda: finish((0, 1), (), (), False, *rest))
     pl.when(place_z() == 1)(lambda: finish((0,), (1,), (), False, *rest))
-    pl.when(place_z() > 1)(lambda: finish((0, 1), (), (), True, *rest))
+    pl.when(place_z() != 1)(lambda: finish((0, 1), (), (), True, *rest))
 
 
 def vmem_spec():

time: 19.7 us -> 19.2 us (0.975)
  Pallas kernels: 11.5 us -> 10.3 us
  waiting for transfers between devices: 0.01 us -> 0.68 us
    pallas_call x6, Pallas kernels: 11.5 us -> 10.3 us  [call(): pl.pallas_call(kernel, out_shape=outs, in_specs=[any_spec() if value.ndim...]
    ppermute x4, waiting for transfers between devices: 0.01 us -> 0.68 us  [swap(): return lax.ppermute(value, axis, pairs + [(j, i) for i, j in pairs])]
  transfers between devices with their start and end apart: 4 -> 4, of which waited for: 0 -> 2; matrix products, arithmetic and copies ran while one was open for 0% -> 0% of each run, Pallas kernels for 8% -> 1%
where the time goes in v10:
time: 19.2 us; the launch traced here: 19.1 us
  Pallas kernels  10.3 us (54%)
  starting transfers between devices  8.06 us (42%)
  waiting for transfers between devices  0.68 us (4%)
    pallas_call x6, Pallas kernels, call(): pl.pallas_call(kernel, out_shape=outs, in_specs=[any_spec() if value.ndim...  10.3 us
    ppermute x4, starting transfers between devices, swap(): return lax.ppermute(value, axis, pairs + [(j, i) for i, j in pairs])  8.06 us
    ppermute x4, waiting for transfers between devices, swap(): return lax.ppermute(value, axis, pairs + [(j, i) for i, j in pairs])  0.68 us
  transfers between devices with their start and end apart: 4, of which 2 were waited for; matrix products, arithmetic and copies ran while one was open for 0% of the time, Pallas kernels for 1%

profile of v10, /device:TPU:1, one launch (start us, length us, event | category | flops | bytes accessed | tf_op | source)
XLA Modules:
  0.0 19.1 jit_solution(5406702398843791201)
XLA Ops:
  0.0 3.1 %pack.1 = (f32[4,2,1576,128]{3,2,1,0:T(8,128)S(1)}, f32[1,2,1544,128]{3,2,1,0:T(8,128)S(1)}, f32[8,256]{1,0:T(8,128)S(1)}, f32[8,256]{1,0:T(8,128)S(1)}, f32[152,128]{1,0:T(8,128)S(1)}, /*index=5*/f32[160,128]{1,0:T(8,128)S(1)}) custom-call(f32[4,1536,256]{2,1,0:T(8,128)} %v_hbm.1), custom_call_target="tpu_custom_call" | custom-call | tf_op jit(solution)/shard_map/pack/pallas_call | solution.py:305
  3.2 3.8 %first.1 = (f32[4,2,1544,128]{3,2,1,0:T(8,128)S(1)}, f32[160,128]{1,0:T(8,128)S(1)}) custom-call(f32[4,2,1576,128]{3,2,1,0:T(8,128)S(1)} %get-tuple-element.17.pad, f32[1,2,1544,128]{3,2,1,0:T(8,128)S(1)} %get-tuple-element.18.z_part, f32[160,128]{1,0:T(8,128)S(1)} %get-tuple-element.19.far_z_in), custom_call_target="tpu_custom_call", output_to_operand_aliasing={{1}: (2, {})} | custom-call | tf_op jit(solution)/shard_map/first/pallas_call | solution.py:305
  6.9 4.9 %collective-permute-start = (f32[160,128]{1,0:T(8,128)S(1)}, f32[160,128]{1,0:T(8,128)S(1)}, u32[]{:S(2)}, u32[]{:S(2)}) collective-permute-start(f32[160,128]{1,0:T(8,128)S(1)} %get-tuple-element.25), channel_id=1, source_target_pairs={{1,2},{3,4},{5,6},{7,8},{9,10},{11,12},{13,14},{15,16},{17,18},{19... | collective-permute-start | bytes 245768 | tf_op jit(solution)/shard_map/ppermute | solution.py:342
  11.9 0.0 collective-permute-start.1
  11.9 2.2 %collective-permute-start.2 = (f32[8,256]{1,0:T(8,128)S(1)}, f32[8,256]{1,0:T(8,128)S(1)}, u32[]{:S(2)}, u32[]{:S(2)}) collective-permute-start(f32[8,256]{1,0:T(8,128)S(1)} %get-tuple-element.27), channel_id=1, source_target_pairs={{32,64},{96,128},{160,192},{224,0},{64,32},{128,96},{192,160},{0,2... | collective-permute-start | bytes 24584 | tf_op jit(solution)/shard_map/ppermute | solution.py:342
  14.0 1.0 %collective-permute-start.3 = (f32[8,256]{1,0:T(8,128)S(1)}, f32[8,256]{1,0:T(8,128)S(1)}, u32[]{:S(2)}, u32[]{:S(2)}) collective-permute-start(f32[8,256]{1,0:T(8,128)S(1)} %get-tuple-element.28), channel_id=1, source_target_pairs={{0,32},{64,96},{128,160},{192,224},{32,0},{96,64},{160,128},{224,1... | collective-permute-start | bytes 24584 | tf_op jit(solution)/shard_map/ppermute | solution.py:342
  15.0 0.0 collective-permute-done.far_z
  15.0 0.1 half.1
  15.2 0.2 %collective-permute-done.2.far_x = f32[8,256]{1,0:T(8,128)S(1)} collective-permute-done((f32[8,256]{1,0:T(8,128)S(1)}, f32[8,256]{1,0:T(8,128)S(1)}, u32[]{:S(2)}, u32[]{:S(2)}) %collective-permute-start.2) | collective-permute-done | bytes 8224 | tf_op jit(solution)/shard_map/ppermute | solution.py:342
  15.4 0.5 %collective-permute-done.3.near_x = f32[8,256]{1,0:T(8,128)S(1)} collective-permute-done((f32[8,256]{1,0:T(8,128)S(1)}, f32[8,256]{1,0:T(8,128)S(1)}, u32[]{:S(2)}, u32[]{:S(2)}) %collective-permute-start.3) | collective-permute-done | bytes 8224 | tf_op jit(solution)/shard_map/ppermute | solution.py:342
  15.8 0.0 collective-permute-done.1.near_z
  15.8 3.3 %edges.1 = f32[4,1536,256]{2,1,0:T(8,128)} custom-call(f32[4,2,1576,128]{3,2,1,0:T(8,128)S(1)} %get-tuple-element.17.pad, f32[4,2,1544,128]{3,2,1,0:T(8,128)S(1)} %inner.1, f32[160,128]{1,0:T(8,128)S(1)} %collective-permute-done.far_z, f32[152,128]{1,0:T(8,128)S(1)} %collective-permute-done.1.near_z, ...), custom_call_target="tpu_custom_call", output_to_operand_aliasing={{}: (6, {})} | custom-call | tf_op jit(solution)/shard_map/edges/pallas_call | solution.py:305
  (2 shorter events, 0.0 us)
Async XLA Ops:
  6.9 8.1 %collective-permute-start = (f32[160,128]{1,0:T(8,128)S(1)}, f32[160,128]{1,0:T(8,128)S(1)}, u32[]{:S(2)}, u32[]{:S(2)}) collective-permute-start(f32[160,128]{1,0:T(8,128)S(1)} %get-tuple-element.25), channel_id=1, source_target_pairs={{1,2},{3,4},{5,6},{7,8},{9,10},{11,12},{13,14},{15,16},{17,18},{19... | collective-permute-start | bytes 245768 | tf_op jit(solution)/shard_map/ppermute | solution.py:342
  11.9 4.0 %collective-permute-start.1 = (f32[152,128]{1,0:T(8,128)S(1)}, f32[152,128]{1,0:T(8,128)S(1)}, u32[]{:S(2)}, u32[]{:S(2)}) collective-permute-start(f32[152,128]{1,0:T(8,128)S(1)} %get-tuple-element.26), channel_id=1, source_target_pairs={{0,1},{2,3},{4,5},{6,7},{8,9},{10,11},{12,13},{14,15},{16,17},{18,... | collective-permute-start | bytes 233480 | tf_op jit(solution)/shard_map/ppermute | solution.py:342
  11.9 3.5 %collective-permute-start.2 = (f32[8,256]{1,0:T(8,128)S(1)}, f32[8,256]{1,0:T(8,128)S(1)}, u32[]{:S(2)}, u32[]{:S(2)}) collective-permute-start(f32[8,256]{1,0:T(8,128)S(1)} %get-tuple-element.27), channel_id=1, source_target_pairs={{32,64},{96,128},{160,192},{224,0},{64,32},{128,96},{192,160},{0,2... | collective-permute-start | bytes 24584 | tf_op jit(solution)/shard_map/ppermute | solution.py:342
  14.0 1.8 %collective-permute-start.3 = (f32[8,256]{1,0:T(8,128)S(1)}, f32[8,256]{1,0:T(8,128)S(1)}, u32[]{:S(2)}, u32[]{:S(2)}) collective-permute-start(f32[8,256]{1,0:T(8,128)S(1)} %get-tuple-element.28), channel_id=1, source_target_pairs={{0,32},{64,96},{128,160},{192,224},{32,0},{96,64},{160,128},{224,1... | collective-permute-start | bytes 24584 | tf_op jit(solution)/shard_map/ppermute | solution.py:342
